TPU v7x, 256 devices: a whole 4x4x8 slice. The times are simulated.
256 devices in a mesh: tm: 8 (over z_lo, core), chan: 32 (over z_hi, x, y).
Axes of the slice: x: 4, y: 4, z: 8 (z_hi: 2, z_lo: 4; z = z_hi * 4 + z_lo), core: 2. Of those that a mesh axis runs over, the one named last changes fastest.
Arguments:
- strain_rate: bfloat16 [2048, 24, 16384], P('chan', 'tm'), may hold values from -600 to 600
- fir_taps: bfloat16 [32], replicated, may hold values from -1 to 1
- source_channels: int32 [128], replicated, may hold values from 0 to 2047
Outputs:
- correlations: float32 [128, 2048, 1024], P(None, ('chan', 'tm'))
Inputs may be any that keep to these rules, and one draw needn't show every extreme that they name: `source_channels`: repeats may occur.
All inputs are finite; a program needn't handle non-finite values.
Results may differ from a plain program's by a relative error of at most 0.0029.
Values may be sent and summed in bfloat16 or wider, within the bound.
A program may use at most 192 MiB of HBM per device.

v0:
```python
import math

import jax
import jax.numpy as jnp
from jax import lax
from jax.sharding import PartitionSpec as P

WIN = 4096
NFREQ = 512
BANDW = 64
K_LO = 32
LAGS = 1024


def forward_table(length, bins, first_bin):
    sample_index = lax.broadcasted_iota(jnp.int32, (length, bins), 0)
    bin_index = lax.broadcasted_iota(jnp.int32, (length, bins), 1) + first_bin
    phases = sample_index * bin_index % (2 * length)
    angles = phases.astype(jnp.float32) * (math.pi / length)
    return jnp.concatenate([jnp.cos(angles), -jnp.sin(angles)], axis=1)


def lag_table(bins, first_bin, length, lag_count):
    bin_index = lax.broadcasted_iota(jnp.int32, (bins, lag_count), 0) + first_bin
    lag_index = lax.broadcasted_iota(jnp.int32, (bins, lag_count), 1) - lag_count // 2 + 2 * length
    phases = bin_index * lag_index % (2 * length)
    angles = phases.astype(jnp.float32) * (math.pi / length)
    return jnp.concatenate([jnp.cos(angles), -jnp.sin(angles)], axis=0)


def whiten(records, fir_taps, table, bins, band_width):
    channels, windows, samples = records.shape
    length = samples // 4
    signal = records.reshape(channels * windows, 1, samples)
    kernel = fir_taps.reshape(1, 1, -1)
    decimated = lax.conv_general_dilated(
        signal, kernel, (4,), [(fir_taps.shape[0] - 1, 0)], preferred_element_type=jnp.float32
    )
    decimated = decimated.reshape(channels * windows, length)
    spectrum = jnp.dot(
        decimated, table, precision=lax.Precision.HIGHEST, preferred_element_type=jnp.float32
    )
    grouped = spectrum.reshape(channels * windows, 2, bins // band_width, band_width)
    band_power = jnp.sum(grouped * grouped, axis=(1, 3), keepdims=True) / band_width
    whitened = grouped * lax.rsqrt(band_power + 1e-06)
    return whitened.reshape(channels, windows, 2, bins).astype(jnp.bfloat16)


def cross_spectra(source_part, local_part):
    src_real = source_part[:, :, 0]
    src_imag = source_part[:, :, 1]
    loc_real = local_part[:, :, 0]
    loc_imag = local_part[:, :, 1]
    pattern = "swk,cwk->sck"
    real_part = jnp.einsum(
        pattern, src_real, loc_real, preferred_element_type=jnp.float32
    ) + jnp.einsum(pattern, src_imag, loc_imag, preferred_element_type=jnp.float32)
    imag_part = jnp.einsum(
        pattern, src_imag, loc_real, preferred_element_type=jnp.float32
    ) - jnp.einsum(pattern, src_real, loc_imag, preferred_element_type=jnp.float32)
    return jnp.stack([real_part, imag_part], axis=2)


def correlate(cross_spec, table, window_total):
    sources, channels, _, bins = cross_spec.shape
    flattened = cross_spec.reshape(sources * channels, 2 * bins)
    result = jnp.dot(
        flattened, table, precision=lax.Precision.HIGHEST, preferred_element_type=jnp.float32
    )
    result = result * (1.0 / math.sqrt(bins * window_total))
    return result.reshape(sources, channels, table.shape[1])


def pick_sources(source_channels, spectra, first_channel):
    channels = spectra.shape[0]
    channel_ids = first_channel + lax.broadcasted_iota(jnp.int32, (1, channels), 1)
    selector = (source_channels[:, None] == channel_ids).astype(jnp.bfloat16)
    flattened = spectra.reshape(channels, -1)
    picked = jnp.dot(selector, flattened, preferred_element_type=jnp.float32)
    return picked.reshape((source_channels.shape[0],) + spectra.shape[1:])


def on_device(strain_rate, fir_taps, source_channels):
    ftable = forward_table(WIN, NFREQ, K_LO)
    spectra = whiten(strain_rate, fir_taps, ftable, NFREQ, BANDW)
    channels = spectra.shape[0]
    windows = spectra.shape[1]
    tm_count = lax.axis_size("tm")
    selection = pick_sources(source_channels, spectra, lax.axis_index("chan") * channels)
    ltable = lag_table(NFREQ, K_LO, WIN, LAGS)
    regrouped = lax.all_to_all(spectra, "tm", split_axis=0, concat_axis=1, tiled=True)
    collected = lax.all_gather(selection.astype(jnp.bfloat16), "tm", axis=1, tiled=True)
    source_part = lax.psum(collected.astype(jnp.float32).astype(jnp.bfloat16), "chan")
    cross_spec = cross_spectra(source_part, regrouped)
    return correlate(cross_spec, ltable, windows * tm_count)


def solution(mesh):
    placed = (P("chan", "tm", None), P(), P())
    return jax.shard_map(
        on_device,
        mesh=mesh,
        in_specs=placed,
        out_specs=P(None, ("chan", "tm"), None),
        check_vma=False,
    )
```

profile of v0, /device:TPU:1, one launch (start us, length us, event | category | flops | bytes accessed | tf_op | source)
XLA Modules:
  0.0 818.2 jit_solution(6208309328843855697)
XLA Ops:
  7.1 36.8 %fusion.10 = (f32[4096,512]{0,1:T(8,128)}, f32[4096,512]{0,1:T(8,128)}) fusion(s32[512]{0:T(512)S(1)} %iota_add_fusion.1), kind=kLoop, calls=%fused_computation.17 | loop fusion | flops 31457280 | bytes 16779264 | tf_op jit(solution)/shard_map/cos | solution.py:20
  43.9 11.4 %copy.26 = bf16[64,3,16384]{2,1,0:T(4,128)(2,1)} copy(bf16[64,3,16384]{2,0,1:T(8,128)(2,1)} %param.3) | data formatting | bytes 12582912 | tf_op args[0]
  55.3 10.2 %reshape.38 = bf16[192,1,16384]{2,0,1:T(8,128)(2,1)} reshape(bf16[64,3,16384]{2,1,0:T(4,128)(2,1)} %copy.26) | data formatting | bytes 12582912 | tf_op jit(solution)/shard_map/reshape | solution.py:34
  65.5 34.1 %copy.27 = bf16[192,1,16384]{0,1,2:T(2,128)(2,1)} copy(bf16[192,1,16384]{2,0,1:T(8,128)(2,1)} %reshape.38) | data formatting | bytes 12582912 | tf_op jit(solution)/shard_map/reshape | solution.py:34
  99.7 56.6 %fusion.34 = f32[192,1,4096]{0,1,2:T(1,128)} fusion(bf16[192,1,16384]{0,1,2:T(2,128)(2,1)} %copy.27, bf16[1,1,32]{1,0,2:T(2,128)(2,1)S(1)} %copy.28), kind=kOutput, calls=%fused_computation.56 | convolution fusion | flops 50279424 | bytes 9437248 | tf_op jit(solution)/shard_map/conv_general_dilated | solution.py:36
  156.3 9.3 %copy.29 = f32[192,1,4096]{2,0,1:T(8,128)S(1)} copy(f32[192,1,4096]{0,1,2:T(1,128)} %fusion.34) | data formatting | bytes 6291456 | tf_op jit(solution)/shard_map/conv_general_dilated | solution.py:36
  165.7 7.0 pad_maximum_fusion
  172.7 14.2 %multiply_reduce_fusion = (f32[192,8]{0,1:T(8,128)S(1)}, f32[192,2,8,64]{0,3,2,1:T(8,128)S(1)}) fusion(f32[2,8,64,4096]{3,2,1,0:T(8,128)S(1)} %bitcast.68, f32[192,1,4096]{2,0,1:T(8,128)S(1)} %copy.29), kind=kOutput, calls=%fused_computation.44 | convolution fusion | flops 9664067584 | bytes 20715520 | tf_op jit(solution)/shard_map/dot_general | solution.py:40
  188.5 1.4 convolution_convert_fusion
  189.9 75.9 %all-gather.2.cloned.1.call-done = bf16[128,24,2,512]{3,0,2,1:T(8,128)(2,1)} async-done(((bf16[128,3,2,512]{3,0,2,1:T(8,128)(2,1)}), bf16[128,24,2,512]{3,0,2,1:T(8,128)(2,1)}) %all-gather.2.cloned.1.call-update) | async-done | bytes 6291472 | tf_op jit(solution)/shard_map/all_gather | solution.py:92
  265.8 9.1 %copy.35 = bf16[128,24,2,512]{0,1,3,2:T(8,128)(2,1)} copy(bf16[128,24,2,512]{3,0,2,1:T(8,128)(2,1)} %all-gather.2.cloned.1.call-done) | data formatting | bytes 12582912 | tf_op jit(solution)/shard_map/all_gather | solution.py:92
  275.0 1.1 convert_element_type.28
  276.1 6.4 all-to-all-start
  282.5 9.8 %fusion.26 = (f32[512,1024]{1,0:T(8,128)}, f32[512,1024]{1,0:T(8,128)}) fusion(s32[1024]{0:T(1024)S(1)} %iota_add_fusion, s32[512]{0:T(512)S(1)} %copy-done.3), kind=kLoop, calls=%fused_computation.42 | loop fusion | flops 7864320 | bytes 4200448 | tf_op jit(solution)/shard_map/cos | solution.py:28
  292.3 5.2 all-to-all-done
  297.6 0.8 copy.40
  299.3 479.3 %all-reduce.2.cloned.1.call-done = bf16[128,24,2,512]{0,1,3,2:T(8,128)(2,1)} async-done(((bf16[128,24,2,512]{0,1,3,2:T(8,128)(2,1)}), bf16[128,24,2,512]{0,1,3,2:T(8,128)(2,1)}) %all-reduce.2.cloned.1.call-update) | async-done | bytes 6291472 | tf_op jit(solution)/shard_map/psum | solution.py:93
  778.6 3.1 fusion.14
  782.4 1.2 fusion.13
  783.5 1.2 add_bitcast_fusion
  784.7 1.2 subtract_bitcast_fusion
  785.9 2.3 pad_maximum_fusion.1
  788.2 5.8 copy.42
  794.0 17.4 %multiply_bitcast_fusion = f32[128,8,1024]{2,1,0:T(8,128)} fusion(f32[1024,1024]{1,0:T(8,128)} %bitcast.69, f32[512,1024]{1,0:T(8,128)} %get-tuple-element.8, f32[512,1024]{1,0:T(8,128)S(1)} %copy-done.1), kind=kOutput, calls=%fused_computation.16 | convolution fusion | flops 12886999040 | bytes 12582912 | tf_op jit(solution)/shard_map/dot_general | solution.py:67
  (28 shorter events, 3.9 us)
Async XLA Ops:
  6.5 259.3 %all-gather.2.cloned.1.call-start = ((), (), s32[]{:S(2)}) async-start(), calls=%async_computation.1 | async-start | bytes 7077888 | tf_op jit(solution)/shard_map/all_gather | solution.py:92
  6.5 0.5 copy-start.2
  65.5 34.1 %copy-start.5 = (bf16[32]{0:T(256)(128)(2,1)S(1)}, bf16[32]{0:T(256)(128)(2,1)}, u32[]{:S(2)}) copy-start(bf16[32]{0:T(256)(128)(2,1)} %param.4) | copy-start | bytes 196
  186.8 1.6 copy-start.4
  189.9 588.8 %all-reduce.2.cloned.1.call-start = ((), (), s32[]{:S(2)}) async-start(), calls=%async_computation.2 | async-start | bytes 12582912 | tf_op jit(solution)/shard_map/psum | solution.py:93
  274.9 7.6 copy-start.3
  276.1 21.5 %all-to-all-start = ((bf16[64,3,2,512]{3,2,1,0:T(2,128)(2,1)}), bf16[64,3,2,512]{3,2,1,0:T(2,128)(2,1)S(1)}, u32[]{:S(2)}, u32[]{:S(2)}) async-start(bf16[64,3,2,512]{3,2,1,0:T(2,128)(2,1)} %convert_element_type.28), calls=%async_computation | async-start | bytes 786432 | tf_op jit(solution)/shard_map/all_to_all | solution.py:91
  778.6 3.7 copy-start
  788.2 5.8 copy-start.1
Sparse Core Ops, SparseCore 0:
  190.0 75.7 all-gather.1
  275.1 503.5 all-reduce.1
where the time goes:
time: 826 us; the launch traced here: 818 us
  waiting for transfers between devices  560 us (68%)
  matrix products  96.1 us (12%)
  local copies, waits for them, and re-layouts  85.6 us (10%)
  other arithmetic  56.1 us (7%)
  between operations  13.5 us (2%)
    psum x1, waiting for transfers between devices, on_device(): lax.psum(collected.astype(jnp.float32).astype(jnp.bfloat16), 'chan')  479 us
    all_gather x1, waiting for transfers between devices, on_device(): lax.all_gather(selection.astype(jnp.bfloat16), 'tm', axis=1, tiled=True)  75.9 us
    conv_general_dilated x1, matrix products, whiten(): lax.conv_general_dilated(signal, kernel, (4,), [(fir_taps.shape[0] - 1, 0...  56.6 us
    reshape x2, local copies, waits for them, and re-layouts, whiten(): signal = records.reshape(channels * windows, 1, samples)  44.3 us
    cos x1, other arithmetic, forward_table(): return jnp.concatenate([jnp.cos(angles), -jnp.sin(angles)], axis=1)  36.8 us
    unnamed x16, local copies, waits for them, and re-layouts  20.1 us
    dot_general x1, matrix products, correlate(): jnp.dot(flattened, table, precision=lax.Precision.HIGHEST, preferred_elem...  17.4 us
  transfers between devices with their start and end apart: 3, of which 3 were waited for; matrix products, arithmetic and copies ran while one was open for 2% of the time, Pallas kernels for 0%

commit v1 on v0

v1 whole, which is shorter than its diff:
```python
import functools
import math

import jax
import jax.numpy as jnp
import ml_dtypes
import numpy as np
from jax import lax
from jax.experimental import pallas as pl
from jax.experimental.pallas import tpu as pltpu
from jax.sharding import PartitionSpec as P

WIN = 4096
NFREQ = 512
BANDW = 64
K_LO = 32
LAGS = 1024
TAPS = 32
NW = 24
SRC = 128
BLK = 512
BF = jnp.bfloat16
F32 = jnp.float32
MESH = pl.DeviceIdType.MESH
VLIM = 56 * 1024 * 1024


def split_bf16(a):
    hi = a.astype(ml_dtypes.bfloat16)
    lo = (a - hi.astype(np.float64)).astype(ml_dtypes.bfloat16)
    return hi, lo


def dft_tables():
    a = np.arange(BLK)[:, None]
    k = np.arange(NFREQ)[None, :] + K_LO
    ang = 2 * np.pi * ((a * k) % (2 * WIN)) / (2 * WIN)
    return split_bf16(np.concatenate([np.cos(ang), -np.sin(ang)], axis=1))


def twiddles():
    b = np.arange(WIN // BLK)[:, None]
    kk = np.arange(256)[None, :]
    ang = 2 * np.pi * ((b * kk * BLK) % (2 * WIN)) / (2 * WIN)
    return np.stack([np.cos(ang), np.sin(ang)], axis=1).astype(np.float32)


def lag_table():
    k = np.arange(NFREQ)[:, None] + K_LO
    i = np.arange(LAGS)[None, :] - LAGS // 2 + 2 * WIN
    ang = 2 * np.pi * ((k * i) % (2 * WIN)) / (2 * WIN)
    t = np.stack([np.cos(ang), -np.sin(ang)]) / math.sqrt(NFREQ * NW)
    t = t.reshape(2, 2, 256, LAGS).transpose(1, 0, 2, 3)
    return t.reshape(2 * NFREQ, LAGS).astype(ml_dtypes.bfloat16)


def band_ones():
    g = np.arange(256) // BANDW
    return (g[:, None] == g[None, :]).astype(ml_dtypes.bfloat16)


def toeplitz(taps):
    d = lax.broadcasted_iota(jnp.int32, (640, 128), 0) - 4 * lax.broadcasted_iota(jnp.int32, (640, 128), 1) - 97
    t = jnp.zeros((640, 128), BF)
    for j in range(TAPS):
        t = jnp.where(d == j, taps[j], t)
    z = jnp.zeros((512, 128), BF)
    return jnp.concatenate([jnp.concatenate([t, z], 0), jnp.concatenate([z, t], 0)], 1)


def dotf(a, b):
    return jnp.dot(a, b, preferred_element_type=F32)


def tdot(a, b):
    return lax.dot_general(a, b, (((0,), (0,)), ((), ())), preferred_element_type=F32)


def hilo(v):
    hi = v.astype(BF)
    return hi, (v - hi.astype(F32)).astype(BF)


def spectra_kernel(x_ref, t_ref, thi_ref, tlo_ref, tw_ref, ones_ref, sel_ref, wst_ref, p_ref, lhs, dhi, dlo):
    rows = x_ref.shape[1]
    lhs[0:rows, 0:128] = jnp.zeros((rows, 128), BF)
    lhs[0:rows, 128:1152] = x_ref[0, :, 0:1024]
    for b in range(1, 16):
        lhs[b * rows:(b + 1) * rows, :] = x_ref[0, :, 1024 * b - 128:1024 * b + 1024]
    d = dotf(lhs[...], t_ref[...])
    for b in range(16):
        hi, lo = hilo(d[b * rows:(b + 1) * rows])
        r0, c0 = (b // 2) * rows, (b % 2) * 256
        dhi[r0:r0 + rows, c0:c0 + 256] = hi
        dlo[r0:r0 + rows, c0:c0 + 256] = lo

    def dot3(c0):
        cols = slice(c0, c0 + 256)
        return dotf(dhi[...], thi_ref[:, cols]) + dotf(dlo[...], thi_ref[:, cols]) + dotf(dhi[...], tlo_ref[:, cols])

    for h in range(2):
        yre = dot3(h * 256)
        yim = dot3(512 + h * 256)
        xre = yre[0:rows]
        xim = yim[0:rows]
        for b in range(1, WIN // BLK):
            c = tw_ref[b, 0:1, :]
            s = tw_ref[b, 1:2, :]
            br = yre[b * rows:(b + 1) * rows]
            bi = yim[b * rows:(b + 1) * rows]
            xre = xre + (br * c + bi * s)
            xim = xim + (bi * c - br * s)
        phi, plo = hilo(xre * xre + xim * xim)
        power = dotf(phi, ones_ref[...]) + dotf(plo, ones_ref[...])
        scale = lax.rsqrt(power * (1.0 / BANDW) + 1e-6)
        wre = (xre * scale).astype(BF)
        wim = (xim * scale).astype(BF)
        for z in range(4):
            wst_ref[h, z, 0, :, 0:256] = wre[16 * z:16 * z + 16]
            wst_ref[h, z, 0, :, 256:512] = wim[16 * z:16 * z + 16]
        for p, part in enumerate((wre, wim)):
            picked = tdot(part, sel_ref[...]).astype(BF)
            for j in range(16):
                p_ref[j, h, 0, p] = picked[16 * j:16 * j + 16]


def spectra(x, toep, sel):
    thi, tlo = dft_tables()
    full = lambda *s: pl.BlockSpec(s, lambda w: (0,) * len(s))
    return pl.pallas_call(
        spectra_kernel,
        grid=(3,),
        in_specs=[
            pl.BlockSpec((1, 64, 4 * WIN), lambda w: (w, 0, 0)),
            full(1152, 256), full(BLK, 1024), full(BLK, 1024), full(8, 2, 256), full(256, 256), full(64, SRC),
        ],
        out_specs=[
            pl.BlockSpec((2, 4, 1, 16, 512), lambda w: (0, 0, w, 0, 0)),
            pl.BlockSpec((16, 2, 1, 2, 16, SRC), lambda w: (0, 0, w, 0, 0, 0)),
        ],
        out_shape=[
            jax.ShapeDtypeStruct((2, 4, 3, 16, 512), BF),
            jax.ShapeDtypeStruct((16, 2, 3, 2, 16, SRC), BF),
        ],
        scratch_shapes=[
            pltpu.VMEM((1024, 1152), BF),
            pltpu.VMEM((512, BLK), BF),
            pltpu.VMEM((512, BLK), BF),
        ],
        compiler_params=pltpu.CompilerParams(vmem_limit_bytes=VLIM),
        name="spectra",
    )(x, toep, jnp.asarray(thi), jnp.asarray(tlo), jnp.asarray(twiddles()), jnp.asarray(band_ones()), sel)


def exchange_kernel(p_ref, wst_ref, s_ref, l_ref, rs, red, zin, rs_send, rs_recv, z_sem, t_send, t_recv,
                    l_send, l_recv, g_send, g_recv, loc):
    m = lax.axis_index("tm")
    ch = lax.axis_index("chan")
    core = m % 2
    zh, xy = ch // 16, ch % 16
    x, y = xy // 4, xy % 4
    barrier = pltpu.get_barrier_semaphore()

    def xy_peer(dx, dy):
        return ((x + dx) % 4) * 4 + (y + dy) % 4

    offs = [(dx, dy) for dx in range(4) for dy in range(4)][1:]
    for dx, dy in offs:
        pl.semaphore_signal(barrier, inc=1, device_id=(m, zh * 16 + xy_peer(dx, dy)), device_id_type=MESH)
    for o in range(1, 8):
        pl.semaphore_signal(barrier, inc=1, device_id=((m + o) % 8, ch), device_id_type=MESH)
    other = (m, (1 - zh) * 16 + xy)
    pl.semaphore_signal(barrier, inc=1, device_id=other, device_id_type=MESH)
    pl.semaphore_wait(barrier, 23)

    def remote(src, dst, ssem, rsem, dev):
        c = pltpu.make_async_remote_copy(src_ref=src, dst_ref=dst, send_sem=ssem, recv_sem=rsem,
                                         device_id=dev, device_id_type=MESH)
        c.start()
        return c

    rs_c = []
    for n, (dx, dy) in enumerate(offs):
        j = xy_peer(dx, dy)
        rs_c.append(remote(p_ref.at[j], rs.at[n], rs_send.at[n], rs_recv.at[n], (m, zh * 16 + j)))
    l_c = []
    for o in range(1, 8):
        mm = (m + o) % 8
        l_c.append(remote(wst_ref.at[mm % 2, mm // 2], l_ref.at[m], l_send.at[o], l_recv.at[o], (mm, ch)))
    own = pltpu.make_async_copy(wst_ref.at[core, m // 2], l_ref.at[m], loc)
    own.start()
    total = p_ref[xy]
    for n in range(15):
        rs_c[n].wait_recv()
        total = total + rs[n]
    red[0] = total
    zc = remote(red.at[0], zin, z_sem.at[0], z_sem.at[1], other)
    zc.wait_recv()
    red[1] = red[0] + zin[...]
    t_c = []
    for o in range(1, 8):
        mm = (m + o) % 8
        t_c.append(remote(red.at[1, mm % 2], s_ref.at[xy, m], t_send.at[o], t_recv.at[o], (mm, ch)))
    s_ref[xy, m] = red[1, core]
    for o in range(1, 8):
        t_c[o - 1].wait_recv()
    own.wait()

    def peer(f, d):
        return zh * 16 + (xy_peer(d, 0) if f == 0 else xy_peer(0, d))

    first = {}
    for f in range(2):
        for d in (1, 3, 2):
            part = s_ref.at[xy, pl.ds(4 * f, 4)]
            first[f, d] = remote(part, part, g_send.at[f, 0, d], g_recv.at[f, 0, d], (m, peer(f, d)))
    second = {}
    for e in (0, 1, 3, 2):
        for f in range(2):
            if e:
                first[f, e].wait_recv()
            src = xy_peer(4 - e, 0) if f == 0 else xy_peer(0, 4 - e)
            for d in (1, 3, 2):
                part = s_ref.at[src, pl.ds(4 * f, 4)]
                second[f, e, d] = remote(part, part, g_send.at[f, 1 + e, d], g_recv.at[f, 1 + e, d],
                                         (m, peer(1 - f, d)))
    for c in second.values():
        c.wait_recv()
    for c in l_c:
        c.wait_recv()
    for c in rs_c + l_c + t_c + [zc] + list(first.values()) + list(second.values()):
        c.wait_send()


def exchange(picks, wst):
    vm = pl.BlockSpec(memory_space=pltpu.VMEM)
    dma = pltpu.SemaphoreType.DMA
    return pl.pallas_call(
        exchange_kernel,
        in_specs=[vm, vm],
        out_specs=[vm, vm],
        out_shape=[
            jax.ShapeDtypeStruct((16, 8, 3, 2, 16, SRC), BF),
            jax.ShapeDtypeStruct((8, 3, 16, 512), BF),
        ],
        scratch_shapes=[
            pltpu.VMEM((15, 2, 3, 2, 16, SRC), BF),
            pltpu.VMEM((2, 2, 3, 2, 16, SRC), BF),
            pltpu.VMEM((2, 3, 2, 16, SRC), BF),
            dma((15,)), dma((15,)), dma((2,)), dma((8,)), dma((8,)), dma((8,)), dma((8,)),
            dma((2, 5, 4)), dma((2, 5, 4)), dma,
        ],
        compiler_params=pltpu.CompilerParams(collective_id=0, has_side_effects=True, vmem_limit_bytes=VLIM),
        name="exchange",
    )(picks, wst)


def cross_kernel(s_ref, l_ref, xf_ref, l32, lt32, lt, a32, x32, xs, send_sem, recv_sem):
    m = lax.axis_index("tm")
    ch = lax.axis_index("chan")
    core = m % 2
    other = (m + 1 - 2 * core, ch)
    barrier = pltpu.get_barrier_semaphore()
    pl.semaphore_signal(barrier, inc=1, device_id=other, device_id_type=MESH)
    l32[...] = l_ref[...].reshape(24, 16, 512).astype(F32)
    for c in range(16):
        mat = l32[:, c, :]
        re, im = mat[:, 0:256], mat[:, 256:512]
        lt32[:, 2 * c, 0:48] = jnp.concatenate([re, im], 0).T
        lt32[:, 2 * c + 1, 0:48] = jnp.concatenate([-im, re], 0).T
    lt[...] = lt32[:, :, 0:48].astype(BF)

    def step(j, carry):
        for w in range(24):
            for p in range(2):
                a32[:, p * 24 + w, :] = s_ref[j, w // 3, w % 3, p].astype(F32)
        for kk in range(16):
            o = dotf(lt[j * 16 + kk], a32[kk].astype(BF))
            x32[:, j * 16 + kk, :] = o
        return carry

    lax.fori_loop(0, 16, step, 0)
    xs[...] = x32[...].astype(BF).reshape(2, 16, 256, SRC)
    pl.semaphore_wait(barrier, 1)
    c = pltpu.make_async_remote_copy(src_ref=xs.at[1 - core], dst_ref=xf_ref.at[core], send_sem=send_sem,
                                     recv_sem=recv_sem, device_id=other, device_id_type=MESH)
    c.start()
    xf_ref[core] = xs[core]
    c.wait()


def cross(s, l):
    vm = pl.BlockSpec(memory_space=pltpu.VMEM)
    dma = pltpu.SemaphoreType.DMA
    return pl.pallas_call(
        cross_kernel,
        in_specs=[vm, vm],
        out_specs=vm,
        out_shape=jax.ShapeDtypeStruct((2, 16, 256, SRC), BF),
        scratch_shapes=[
            pltpu.VMEM((24, 16, 512), F32),
            pltpu.VMEM((256, 32, 128), F32),
            pltpu.VMEM((256, 32, 48), BF),
            pltpu.VMEM((16, 48, SRC), F32),
            pltpu.VMEM((32, 256, SRC), F32),
            pltpu.VMEM((2, 16, 256, SRC), BF),
            dma, dma,
        ],
        compiler_params=pltpu.CompilerParams(collective_id=1, has_side_effects=True, vmem_limit_bytes=VLIM),
        name="cross",
    )(s, l)


def lags_kernel(xf_ref, lt_ref, out_ref):
    for c in range(8):
        a = xf_ref[:, 2 * c:2 * c + 2].reshape(1024, SRC)
        out_ref[:, c, :] = tdot(a, lt_ref[...])


def lags(xf):
    vm = pl.BlockSpec(memory_space=pltpu.VMEM)
    return pl.pallas_call(
        lags_kernel,
        in_specs=[vm, vm],
        out_specs=vm,
        out_shape=jax.ShapeDtypeStruct((SRC, 8, LAGS), F32),
        compiler_params=pltpu.CompilerParams(vmem_limit_bytes=VLIM),
        name="lags",
    )(xf, jnp.asarray(lag_table()))


def on_device(strain_rate, fir_taps, source_channels):
    x = jnp.transpose(strain_rate, (1, 0, 2))
    first = lax.axis_index("chan") * 64
    ids = first + lax.broadcasted_iota(jnp.int32, (64, SRC), 0)
    sel = (ids == source_channels[None, :]).astype(BF)
    wst, picks = spectra(x, toeplitz(fir_taps), sel)
    s, l = exchange(picks, wst)
    xf = cross(s, l)
    return lags(xf)


def solution(mesh):
    placed = (P("chan", "tm", None), P(), P())
    return jax.shard_map(
        on_device,
        mesh=mesh,
        in_specs=placed,
        out_specs=P(None, ("chan", "tm"), None),
        check_vma=False,
    )
```

time: 826 us -> 134 us (0.16)
  waiting for transfers between devices: 560 us -> 0 us
  Pallas kernels: 0 us -> 107 us
  matrix products: 96.1 us -> 0 us
  local copies, waits for them, and re-layouts: 85.6 us -> 3.92 us
  other arithmetic: 56.1 us -> 23 us
  between operations: 13.5 us -> 0.04 us
    psum x1 -> x0, waiting for transfers between devices: 479 us -> none  [on_device(): lax.psum(collected.astype(jnp.float32).astype(jnp.bfloat16), 'chan')]
    pallas_call x0 -> x4, Pallas kernels: none -> 107 us  [the longest x1 60.5 us: exchange(): pl.pallas_call(exchange_kernel, in_specs=[vm, vm], out_specs=[vm, vm], ou...]
    all_gather x1 -> x0, waiting for transfers between devices: 75.9 us -> none  [on_device(): lax.all_gather(selection.astype(jnp.bfloat16), 'tm', axis=1, tiled=True)]
    conv_general_dilated x1 -> x0, matrix products: 56.6 us -> none  [whiten(): lax.conv_general_dilated(signal, kernel, (4,), [(fir_taps.shape[0] - 1, 0...]
    cos x2 -> x0, other arithmetic: 46.7 us -> none  [the longest x1 36.8 us: forward_table(): return jnp.concatenate([jnp.cos(angles), -jnp.sin(angles)], axis=1)]
    reshape x3 -> x0, local copies, waits for them, and re-layouts: 44.4 us -> none  [the longest x2 44.3 us: whiten(): signal = records.reshape(channels * windows, 1, samples)]
    dot_general x7 -> x0, matrix products: 39.5 us -> none  [the longest x1 17.4 us: correlate(): jnp.dot(flattened, table, precision=lax.Precision.HIGHEST, preferred_elem...]
    select_n x0 -> x1, other arithmetic: none -> 20.8 us  [toeplitz(): t = jnp.where(d == j, taps[j], t)]
  transfers between devices with their start and end apart: 3 -> 0, of which waited for: 3 -> 0; matrix products, arithmetic and copies ran while one was open for 2% -> 0% of each run, Pallas kernels for 0% -> 0%
where the time goes in v1:
time: 134 us
  Pallas kernels  107 us (80%)
  other arithmetic  23 us (17%)
  local copies, waits for them, and re-layouts  3.92 us (3%)
    pallas_call x1, Pallas kernels, exchange(): pl.pallas_call(exchange_kernel, in_specs=[vm, vm], out_specs=[vm, vm], ou...  60.5 us
    pallas_call x1, Pallas kernels, cross(): pl.pallas_call(cross_kernel, in_specs=[vm, vm], out_specs=vm, out_shape=j...  21.2 us
    select_n x1, other arithmetic, toeplitz(): t = jnp.where(d == j, taps[j], t)  20.8 us
    pallas_call x1, Pallas kernels, spectra(): pl.pallas_call(spectra_kernel, grid=(3,), in_specs=[pl.BlockSpec((1, 64,...  17.5 us
    pallas_call x1, Pallas kernels, lags(): pl.pallas_call(lags_kernel, in_specs=[vm, vm], out_specs=vm, out_shape=ja...  7.71 us
    slice x2, local copies, waits for them, and re-layouts, toeplitz(): t = jnp.where(d == j, taps[j], t)  3.92 us

profile of v1, /device:TPU:1, one launch (start us, length us, event | category | flops | bytes accessed | tf_op | source)
XLA Modules:
  0.0 133.8 jit_solution(17447045527630469854)
XLA Ops:
  0.0 1.8 %fusion.68 = (bf16[1]{0:T(256)(128)(2,1)}, bf16[1]{0:T(256)(128)(2,1)}, bf16[1]{0:T(256)(128)(2,1)}, bf16[1]{0:T(256)(128)(2,1)}, bf16[1]{0:T(256)(128)(2,1)}, /...) fusion(bf16[32]{0:T(256)(128)(2,1)} %param.9), kind=kLoop, calls=%fused_computation.74 | loop fusion | bytes 52 | tf_op jit(solution)/shard_map/slice | solution.py:66
  1.8 2.1 %fusion.67 = (bf16[1]{0:T(256)(128)(2,1)}, bf16[1]{0:T(256)(128)(2,1)}, bf16[1]{0:T(256)(128)(2,1)}, bf16[1]{0:T(256)(128)(2,1)}, bf16[1]{0:T(256)(128)(2,1)}, /...) fusion(bf16[32]{0:T(256)(128)(2,1)} %param.9), kind=kLoop, calls=%fused_computation.73 | loop fusion | bytes 76 | tf_op jit(solution)/shard_map/slice | solution.py:66
  3.9 1.3 compare_convert_fusion.sel_ref
  5.3 20.8 %fusion.35 = bf16[640,128]{1,0:T(8,128)(2,1)S(1)} fusion(s32[128]{0:T(128)S(1)} %iota_multiply_fusion, bf16[]{:T(256)} %bitcast.32, bf16[]{:T(256)} %bitcast.31, bf16[]{:T(256)} %bitcast.30, bf16[]{:T(256)} %bitcast.29, bf16[]{:T(256)} %bitcast.28, bf16[]{:T(256)} %bitcast.27, bf16[]{:T(256)} %bitcast.26, bf16[]{:T(256)} %bitcast.25, bf16[]{:T(256)} %bitcast.24, ...), kind=kLoop, calls=%fused_computation.38 | loop fusion | flops 5406720 | bytes 164416 | tf_op jit(solution)/shard_map/jit(_where)/select_n | solution.py:66
  26.0 0.9 fusion.2.t_ref
  26.9 17.5 %spectra.1 = (bf16[2,4,3,16,512]{4,3,2,1,0:T(8,128)(2,1)}, bf16[16,2,3,2,16,128]{5,4,3,2,1,0:T(8,128)(2,1)}) custom-call(bf16[3,64,16384]{2,1,0:T(8,128)(2,1)} %bitcast.33, bf16[1152,256]{1,0:T(8,128)(2,1)} %fusion.2.t_ref, bf16[512,1024]{1,0:T(8,128)(2,1)} %constant.86.clone.thi_ref, bf16[512,1024]{1,0:T(8,128)(2,1)} %constant.87.clone.tlo_ref, ...), custom_call_target="tpu_custom_call" | custom-call | tf_op jit(solution)/shard_map/spectra/pallas_call | solution.py:130
  44.4 60.5 %exchange.1 = (bf16[16,8,3,2,16,128]{5,4,3,2,1,0:T(8,128)(2,1)}, bf16[8,3,16,512]{3,2,1,0:T(8,128)(2,1)}) custom-call(bf16[16,2,3,2,16,128]{5,4,3,2,1,0:T(8,128)(2,1)} %get-tuple-element.9.p_ref, bf16[2,4,3,16,512]{4,3,2,1,0:T(8,128)(2,1)} %get-tuple-element.10.wst_ref), custom_call_target="tpu_custom_call" | custom-call | tf_op jit(solution)/shard_map/exchange/pallas_call | solution.py:238
  104.9 21.2 %cross.1.xf_ref = bf16[2,16,256,128]{3,2,1,0:T(8,128)(2,1)} custom-call(bf16[16,8,3,2,16,128]{5,4,3,2,1,0:T(8,128)(2,1)} %get-tuple-element.11.s_ref, bf16[8,3,16,512]{3,2,1,0:T(8,128)(2,1)} %get-tuple-element.12.l_ref), custom_call_target="tpu_custom_call" | custom-call | tf_op jit(solution)/shard_map/cross/pallas_call | solution.py:295
  126.1 7.7 %lags.1 = f32[128,8,1024]{2,1,0:T(8,128)} custom-call(bf16[2,16,256,128]{3,2,1,0:T(8,128)(2,1)} %cross.1.xf_ref, bf16[1024,1024]{1,0:T(8,128)(2,1)} %constant.90.clone.lt_ref), custom_call_target="tpu_custom_call" | custom-call | tf_op jit(solution)/shard_map/lags/pallas_call | solution.py:322
  (2 shorter events, 0.0 us)

commit v2 on v1

v2 whole, which is shorter than its diff:
```python
import functools
import math

import jax
import jax.numpy as jnp
import ml_dtypes
import numpy as np
from jax import lax
from jax.experimental import pallas as pl
from jax.experimental.pallas import tpu as pltpu
from jax.sharding import PartitionSpec as P

WIN = 4096
NFREQ = 512
BANDW = 64
K_LO = 32
LAGS = 1024
TAPS = 32
NW = 24
SRC = 128
BLK = 512
BF = jnp.bfloat16
F32 = jnp.float32
MESH = pl.DeviceIdType.MESH
VLIM = 56 * 1024 * 1024


def split_bf16(a):
    hi = a.astype(ml_dtypes.bfloat16)
    lo = (a - hi.astype(np.float64)).astype(ml_dtypes.bfloat16)
    return hi, lo


def dft_tables():
    u = np.arange(256)[:, None] - 255.5
    ang = 2 * np.pi * u * (np.arange(NFREQ)[None, :] + K_LO) / (2 * WIN)
    out = []
    for t in (np.cos(ang), np.sin(ang)):
        hi, lo = split_bf16(t)
        out.append(np.concatenate([hi, hi, lo], axis=0))
    return np.stack(out)


def twiddles():
    t = np.arange(WIN // BLK)[:, None] * BLK + 255.5
    ang = 2 * np.pi * t * (np.arange(NFREQ)[None, :] + K_LO) / (2 * WIN)
    return np.stack([np.cos(ang), np.sin(ang)], axis=1).astype(np.float32)


def tap_spread():
    j, a, l = np.ogrid[0:TAPS, 0:8, 0:128]
    fwd = (l < 10) & (a - 4 * l + 31 == j)
    rev = (l < 10) & (a - 4 * (9 - l) + 31 == j)
    return np.stack([fwd, rev], axis=1).reshape(TAPS, 2048).astype(ml_dtypes.bfloat16)


def lag_table():
    k = np.arange(NFREQ)[:, None] + K_LO
    i = np.arange(LAGS)[None, :] - LAGS // 2 + 2 * WIN
    ang = 2 * np.pi * ((k * i) % (2 * WIN)) / (2 * WIN)
    t = np.stack([np.cos(ang), -np.sin(ang)]) / math.sqrt(NFREQ * NW)
    t = t.reshape(2, 2, 256, LAGS).transpose(1, 0, 2, 3)
    return t.reshape(2 * NFREQ, LAGS).astype(ml_dtypes.bfloat16)


def band_ones():
    g = np.arange(256) // BANDW
    return (g[:, None] == g[None, :]).astype(ml_dtypes.bfloat16)


def dotf(a, b):
    return jnp.dot(a, b, preferred_element_type=F32)


def tdot(a, b):
    return lax.dot_general(a, b, (((0,), (0,)), ((), ())), preferred_element_type=F32)


def hilo(v):
    hi = v.astype(BF)
    return hi, (v - hi.astype(F32)).astype(BF)


def band_rows(unit, start, lane_tile):
    lane = lax.broadcasted_iota(jnp.int32, (8, 128), 1) + 128 * lane_tile
    lo, hi = 128 * lane_tile, 128 * lane_tile + 127
    if start > hi or start + 9 < lo:
        return jnp.zeros((8, 128), F32)
    moved = pltpu.roll(unit, start % 128, 1) if start % 128 else unit
    return jnp.where((lane >= start) & (lane < start + 10), moved, 0.0)


def build_bands(taps, spread, bands):
    row = dotf(taps, spread)
    for v in range(2):
        unit = jnp.concatenate([row[0:1, (8 * v + a) * 128:(8 * v + a + 1) * 128] for a in range(8)], axis=0)
        for r in range(0, 144, 2):
            starts = [(2 * q - 32) if v == 0 else (278 - 2 * q) for q in (r, r + 1)]
            for t in range(2):
                rows = jnp.concatenate([band_rows(unit, s, t) for s in starts], axis=0)
                bands[v, 8 * r:8 * r + 16, 128 * t:128 * t + 128] = rows.astype(BF)


def spectra_kernel(x_ref, taps_ref, spread_ref, tab_ref, tw_ref, ones_ref, sel_ref, wst_ref, p_ref,
                   bands, lhs, dcat):
    rows = 64

    @pl.when(pl.program_id(0) == 0)
    def _():
        build_bands(taps_ref[...], spread_ref[...], bands)

    for b in range(16):
        r0 = (b // 2) * rows
        if b == 0:
            lhs[0, 0:rows, 0:128] = jnp.zeros((rows, 128), BF)
            lhs[0, 0:rows, 128:1152] = x_ref[0, :, 0:1024]
        else:
            lhs[b % 2, r0:r0 + rows, :] = x_ref[0, :, 1024 * b - 128:1024 * b + 1024]
    even = dotf(lhs[0], bands[0])
    odd = dotf(lhs[1], bands[1])
    for i, v in enumerate((even + odd, even - odd)):
        hi, lo = hilo(v)
        dcat[i, :, 0:256] = hi
        dcat[i, :, 256:512] = lo
        dcat[i, :, 512:768] = hi

    for h in range(2):
        cols = slice(256 * h, 256 * h + 256)
        yc = dotf(dcat[0], tab_ref[0, :, cols])
        ys = dotf(dcat[1], tab_ref[1, :, cols])
        xre = xim = 0.0
        for b in range(WIN // BLK):
            c = tw_ref[b, 0:1, cols]
            s = tw_ref[b, 1:2, cols]
            bc = yc[b * rows:(b + 1) * rows]
            bs = ys[b * rows:(b + 1) * rows]
            xre = xre + (bc * c - bs * s)
            xim = xim - (bs * c + bc * s)
        phi, plo = hilo(xre * xre + xim * xim)
        power = dotf(phi, ones_ref[...]) + dotf(plo, ones_ref[...])
        scale = lax.rsqrt(power * (1.0 / BANDW) + 1e-6)
        wre = (xre * scale).astype(BF)
        wim = (xim * scale).astype(BF)
        for z in range(4):
            wst_ref[h, z, 0, :, 0:256] = wre[16 * z:16 * z + 16]
            wst_ref[h, z, 0, :, 256:512] = wim[16 * z:16 * z + 16]
        for p, part in enumerate((wre, wim)):
            picked = tdot(part, sel_ref[...]).astype(BF)
            for j in range(16):
                p_ref[h, j // 4, j % 4, 0, p] = picked[16 * j:16 * j + 16]


def spectra(x, taps, sel):
    full = lambda *s: pl.BlockSpec(s, lambda w: (0,) * len(s))
    return pl.pallas_call(
        spectra_kernel,
        grid=(3,),
        in_specs=[
            pl.BlockSpec((1, 64, 4 * WIN), lambda w: (w, 0, 0)),
            full(1, TAPS), full(TAPS, 2048), full(2, 768, NFREQ), full(8, 2, NFREQ), full(256, 256), full(64, SRC),
        ],
        out_specs=[
            pl.BlockSpec((2, 4, 1, 16, 512), lambda w: (0, 0, w, 0, 0)),
            pl.BlockSpec((2, 4, 4, 1, 2, 16, SRC), lambda w: (0, 0, 0, w, 0, 0, 0)),
        ],
        out_shape=[
            jax.ShapeDtypeStruct((2, 4, 3, 16, 512), BF),
            jax.ShapeDtypeStruct((2, 4, 4, 3, 2, 16, SRC), BF),
        ],
        scratch_shapes=[
            pltpu.VMEM((2, 1152, 256), BF),
            pltpu.VMEM((2, 512, 1152), BF),
            pltpu.VMEM((2, 512, 768), BF),
        ],
        compiler_params=pltpu.CompilerParams(vmem_limit_bytes=VLIM),
        name="spectra",
    )(x, taps, jnp.asarray(tap_spread()), jnp.asarray(dft_tables()), jnp.asarray(twiddles()),
      jnp.asarray(band_ones()), sel)


def swap_blocks(vs):
    lane = lax.broadcasted_iota(jnp.int32, vs[0].shape, 1) // 16
    for bit in (1, 2, 4):
        low = lane & bit == 0
        out = list(vs)
        for i in range(8):
            if i & bit == 0:
                a, b = vs[i], vs[i + bit]
                out[i] = jnp.where(low, a, pltpu.roll(b, 16 * bit, 1))
                out[i + bit] = jnp.where(low, pltpu.roll(a, 128 - 16 * bit, 1), b)
        vs = out
    return vs


def build_left(l_buf, u, left):
    odd = (lax.broadcasted_iota(jnp.int32, (16, 128), 1) // 16) % 2 == 1
    for q in range(2):
        for g in range(6):
            vs = []
            for i in range(8):
                w, p = (8 * g + i) // 2, i % 2
                vs.append(l_buf[w // 3, w % 3, :, 256 * p + 128 * q:256 * p + 128 * q + 128].astype(F32))
            for j, v in enumerate(swap_blocks(vs)):
                turned = jnp.where(odd, pltpu.roll(v, 16, 1), -pltpu.roll(v, 112, 1))
                u[0, 8 * q + j, :, 128 * g:128 * g + 128] = v
                u[1, 8 * q + j, :, 128 * g:128 * g + 128] = turned
    diag = lax.broadcasted_iota(jnp.int32, (16, 768), 1) % 16 == lax.broadcasted_iota(jnp.int32, (16, 768), 0)

    def expand(j, carry):
        for c in range(16):
            for p in range(2):
                row = jnp.broadcast_to(u[p, j, c:c + 1, :], (16, 768))
                r0 = (2 * c + p) * 16
                left[j, r0:r0 + 16, :] = jnp.where(diag, row, 0.0).astype(BF)
        return carry

    lax.fori_loop(0, 16, expand, 0)


def exchange_kernel(p_ref, wst_ref, xf_ref, r1, acc, r2, red, zin, s_buf, l_buf, u, left, xs,
                    r_send, r_recv, z_sem, t_send, t_recv, l_send, l_recv, g_send, g_recv, x_sem, loc):
    m = lax.axis_index("tm")
    ch = lax.axis_index("chan")
    core = m % 2
    zh, xy = ch // 16, ch % 16
    x, y = xy // 4, xy % 4
    barrier = pltpu.get_barrier_semaphore()

    def xy_peer(dx, dy):
        return ((x + dx) % 4) * 4 + (y + dy) % 4

    def along(axis, d):
        return (m, zh * 16 + (xy_peer(d, 0) if axis == 0 else xy_peer(0, d)))

    other_z = (m, (1 - zh) * 16 + xy)
    other_core = (m + 1 - 2 * core, ch)
    for axis in range(2):
        for d in (1, 2, 3):
            pl.semaphore_signal(barrier, inc=1, device_id=along(axis, d), device_id_type=MESH)
    for o in range(1, 8):
        pl.semaphore_signal(barrier, inc=1, device_id=((m + o) % 8, ch), device_id_type=MESH)
    pl.semaphore_signal(barrier, inc=1, device_id=other_z, device_id_type=MESH)
    pl.semaphore_wait(barrier, 14)
    copies = []

    def remote(src, dst, ssem, rsem, dev):
        c = pltpu.make_async_remote_copy(src_ref=src, dst_ref=dst, send_sem=ssem, recv_sem=rsem,
                                         device_id=dev, device_id_type=MESH)
        c.start()
        copies.append(c)
        return c

    def chunk(f, d):
        return p_ref.at[0, (x + d) % 4] if f == 0 else p_ref.at[1, :, (y + d) % 4]

    mine = (x, y)
    got = {}
    for d in (2, 1, 3):
        for f in range(2):
            got[f, d] = remote(chunk(f, d), r1.at[f, d - 1], r_send.at[f, 0, d - 1],
                               r_recv.at[f, 0, d - 1], along(f, d))
    l_c = []
    for o in range(1, 8):
        mm = (m + o) % 8
        l_c.append(remote(wst_ref.at[mm % 2, mm // 2], l_buf.at[m], l_send.at[o], l_recv.at[o], (mm, ch)))
    own = pltpu.make_async_copy(wst_ref.at[core, m // 2], l_buf.at[m], loc)
    own.start()
    got2 = {}
    for f in range(2):
        for d in (1, 3, 2):
            got[f, d].wait_recv()
        acc[f] = chunk(f, 0)[...] + r1[f, 0] + r1[f, 1] + r1[f, 2]
        for d in (2, 1, 3):
            got2[f, d] = remote(acc.at[f, (mine[1 - f] + d) % 4], r2.at[f, d - 1], r_send.at[f, 1, d - 1],
                                r_recv.at[f, 1, d - 1], along(1 - f, d))
    for f in range(2):
        for d in (1, 3, 2):
            got2[f, d].wait_recv()
        red[0, f] = acc[f, mine[1 - f]] + r2[f, 0] + r2[f, 1] + r2[f, 2]
    remote(red.at[0], zin, z_sem.at[0], z_sem.at[1], other_z).wait_recv()
    red[1] = red[0] + zin[...]
    t_c = []
    for o in range(1, 8):
        mm = (m + o) % 8
        t_c.append(remote(red.at[1, mm % 2], s_buf.at[xy, m], t_send.at[o], t_recv.at[o], (mm, ch)))
    s_buf[xy, m] = red[1, core]
    own.wait()
    for c in l_c:
        c.wait_recv()
    build_left(l_buf, u, left)
    for c in t_c:
        c.wait_recv()

    arrived = {}

    def mark(f, a, b, n):
        key = (a, b) if f == 0 else (b, a)
        arrived[key] = arrived.get(key, 0) + n
        if arrived[key] == 4:
            j = xy_peer(*key)
            o = dotf(left[j], s_buf[j].reshape(768, SRC))
            xs[:, j] = o.astype(BF).reshape(32, 16, SRC)

    def shard(f, a, b):
        return xy_peer(a, b) if f == 0 else xy_peer(b, a)

    def send(f, src, first, count, slot, d, axis):
        part = s_buf.at[src, pl.ds(4 * f + first, count)]
        return remote(part, part, g_send.at[f, slot], g_recv.at[f, slot], along(axis, d))

    c1, c2 = {}, {}

    def second(f, a, slot):
        c2[f, a, 1] = send(f, shard(f, a, 0), 0, 4, slot, 1, 1 - f)
        c2[f, a, 3] = send(f, shard(f, a, 0), 0, 4, slot + 1, 3, 1 - f)

    def forward(f, a, slot):
        c2[f, a, 1].wait_recv()
        c2[f, a, 4] = send(f, shard(f, a, 3), 0, 2, slot + 2, 1, 1 - f)
        c2[f, a, 3].wait_recv()
        c2[f, a, 5] = send(f, shard(f, a, 1), 2, 2, slot + 3, 3, 1 - f)

    def finish(f, a):
        c2[f, a, 4].wait_recv()
        c2[f, a, 5].wait_recv()

    for f in range(2):
        c1[f, 1] = send(f, xy, 0, 4, 0, 1, f)
        c1[f, 3] = send(f, xy, 0, 4, 1, 3, f)
    for f in range(2):
        second(f, 0, 4)
    mark(0, 0, 0, 4)
    for f in range(2):
        c1[f, 1].wait_recv()
        c1[f, 4] = send(f, shard(f, 3, 0), 0, 2, 2, 1, f)
        c1[f, 3].wait_recv()
        c1[f, 5] = send(f, shard(f, 1, 0), 2, 2, 3, 3, f)
    for f in range(2):
        second(f, 3, 8)
        second(f, 1, 12)
    for f in range(2):
        forward(f, 0, 4)
    for f in range(2):
        c1[f, 4].wait_recv()
        c1[f, 5].wait_recv()
        second(f, 2, 16)
    for f in range(2):
        for a in (1, 3, 2):
            mark(f, a, 0, 2)
        for b in (1, 3):
            mark(f, 0, b, 2)
    for f in range(2):
        forward(f, 3, 8)
    for f in range(2):
        finish(f, 0)
        mark(f, 0, 2, 2)
    for f in range(2):
        forward(f, 1, 12)
    for f in range(2):
        for a in (1, 3):
            for b in (1, 3):
                mark(f, a, b, 2)
    for f in range(2):
        forward(f, 2, 16)
        mark(f, 2, 1, 2)
        mark(f, 2, 3, 2)
    for a in (3, 1, 2):
        for f in range(2):
            finish(f, a)
            mark(f, a, 2, 2)

    xc = remote(xs.at[pl.ds((1 - core) * 16, 16)], xf_ref.at[core], x_sem.at[0], x_sem.at[1], other_core)
    xf_ref[core] = xs[pl.ds(core * 16, 16)]
    xc.wait_recv()
    for c in copies:
        c.wait_send()


def exchange(picks, wst):
    vm = pl.BlockSpec(memory_space=pltpu.VMEM)
    dma = pltpu.SemaphoreType.DMA
    tile = (3, 2, 16, SRC)
    return pl.pallas_call(
        exchange_kernel,
        in_specs=[vm, vm],
        out_specs=vm,
        out_shape=jax.ShapeDtypeStruct((2, 16, 16, 16, SRC), BF),
        scratch_shapes=[
            pltpu.VMEM((2, 3, 4) + tile, BF),
            pltpu.VMEM((2, 4) + tile, BF),
            pltpu.VMEM((2, 3) + tile, BF),
            pltpu.VMEM((2, 2) + tile, BF),
            pltpu.VMEM((2,) + tile, BF),
            pltpu.VMEM((16, 8) + tile, BF),
            pltpu.VMEM((8, 3, 16, 512), BF),
            pltpu.VMEM((2, 16, 16, 768), F32),
            pltpu.VMEM((16, 512, 768), BF),
            pltpu.VMEM((32, 16, 16, SRC), BF),
            dma((2, 2, 3)), dma((2, 2, 3)), dma((2,)), dma((8,)), dma((8,)), dma((8,)), dma((8,)),
            dma((2, 20)), dma((2, 20)), dma((2,)), dma,
        ],
        compiler_params=pltpu.CompilerParams(collective_id=0, has_side_effects=True, vmem_limit_bytes=VLIM),
        name="exchange",
    )(picks, wst)


def lags_kernel(xf_ref, lt_ref, out_ref, lhs):
    @pl.when(pl.program_id(0) == 0)
    def _():
        for c in range(8):
            lhs[c * SRC:(c + 1) * SRC, :] = xf_ref[:, 2 * c:2 * c + 2].reshape(1024, SRC).T

    o = dotf(lhs[...], lt_ref[...])
    for c in range(8):
        out_ref[:, c, :] = o[c * SRC:(c + 1) * SRC]


def lags(xf):
    return pl.pallas_call(
        lags_kernel,
        grid=(4,),
        in_specs=[
            pl.BlockSpec((2, 16, 256, SRC), lambda n: (0, 0, 0, 0)),
            pl.BlockSpec((1024, 256), lambda n: (0, n)),
        ],
        out_specs=pl.BlockSpec((SRC, 8, 256), lambda n: (0, 0, n)),
        out_shape=jax.ShapeDtypeStruct((SRC, 8, LAGS), F32),
        scratch_shapes=[pltpu.VMEM((1024, 1024), BF)],
        compiler_params=pltpu.CompilerParams(vmem_limit_bytes=VLIM),
        name="lags",
    )(xf, jnp.asarray(lag_table()))


def on_device(strain_rate, fir_taps, source_channels):
    x = jnp.transpose(strain_rate, (1, 0, 2))
    first = lax.axis_index("chan") * 64
    ids = first + lax.broadcasted_iota(jnp.int32, (64, SRC), 0)
    sel = (ids == source_channels[None, :]).astype(BF)
    wst, picks = spectra(x, fir_taps.reshape(1, TAPS), sel)
    xf = exchange(picks, wst)
    return lags(xf.reshape(2, 16, 256, SRC))


def solution(mesh):
    placed = (P("chan", "tm", None), P(), P())
    return jax.shard_map(
        on_device,
        mesh=mesh,
        in_specs=placed,
        out_specs=P(None, ("chan", "tm"), None),
        check_vma=False,
    )
```

time: 134 us -> 76.9 us (0.57)
  Pallas kernels: 107 us -> 75.4 us
  other arithmetic: 23 us -> 1.33 us
  local copies, waits for them, and re-layouts: 3.92 us -> 0 us
    pallas_call x3 -> x2, Pallas kernels: 89.3 us -> 64.5 us  [the longest x1 57.2 us: exchange(): pl.pallas_call(exchange_kernel, in_specs=[vm, vm], out_specs=vm, out_shap...]
    select_n x1 -> x0, other arithmetic: 20.8 us -> none  [toeplitz(): t = jnp.where(d == j, taps[j], t)]
    pallas_call x1, Pallas kernels: 17.5 us -> 10.9 us  [spectra(): pl.pallas_call(spectra_kernel, grid=(3,), in_specs=[pl.BlockSpec((1, 64,...]
    slice x2 -> x0, local copies, waits for them, and re-layouts: 3.92 us -> none  [toeplitz(): t = jnp.where(d == j, taps[j], t)]
where the time goes in v2:
time: 76.9 us; the launch traced here: 76.7 us
  Pallas kernels  75.4 us (98%)
  other arithmetic  1.33 us (2%)
    pallas_call x1, Pallas kernels, exchange(): pl.pallas_call(exchange_kernel, in_specs=[vm, vm], out_specs=vm, out_shap...  57.2 us
    pallas_call x1, Pallas kernels, spectra(): pl.pallas_call(spectra_kernel, grid=(3,), in_specs=[pl.BlockSpec((1, 64,...  10.9 us
    pallas_call x1, Pallas kernels, lags(): pl.pallas_call(lags_kernel, grid=(4,), in_specs=[pl.BlockSpec((2, 16, 256...  7.27 us

profile of v2, /device:TPU:1, one launch (start us, length us, event | category | flops | bytes accessed | tf_op | source)
XLA Modules:
  0.0 76.7 jit_solution(4437507935786177699)
XLA Ops:
  0.0 1.3 %compare_convert_fusion.sel_ref = bf16[64,128]{1,0:T(8,128)(2,1)} fusion(s32[128]{0:T(128)} %param.10, s32[64]{0:T(128)S(1)} %iota_add_fusion), kind=kLoop, calls=%fused_computation | loop fusion | flops 16384 | bytes 17152 | tf_op jit(solution)/shard_map/convert_element_type | solution.py:438
  1.3 10.9 %spectra.1 = (bf16[2,4,3,16,512]{4,3,2,1,0:T(8,128)(2,1)}, bf16[2,4,4,3,2,16,128]{6,5,4,3,2,1,0:T(8,128)(2,1)}) custom-call(bf16[3,64,16384]{2,1,0:T(8,128)(2,1)} %bitcast.4, bf16[1,32]{1,0:T(2,128)(2,1)} %bitcast.5, bf16[32,2048]{1,0:T(8,128)(2,1)} %constant.16.clone.spread_ref, bf16[2,768,512]{2,1,0:T(8,128)(2,1)} %constant.17.clone.tab_ref, ...), custom_call_target="tpu_custom_call" | custom-call | tf_op jit(solution)/shard_map/spectra/pallas_call | solution.py:155
  12.2 57.2 %exchange.1 = bf16[2,16,16,16,128]{4,3,2,1,0:T(8,128)(2,1)} custom-call(bf16[2,4,4,3,2,16,128]{6,5,4,3,2,1,0:T(8,128)(2,1)} %get-tuple-element.7.p_ref, bf16[2,4,3,16,512]{4,3,2,1,0:T(8,128)(2,1)} %get-tuple-element.8.wst_ref), custom_call_target="tpu_custom_call" | custom-call | tf_op jit(solution)/shard_map/exchange/pallas_call | solution.py:383
  69.4 7.3 %lags.1 = f32[128,8,1024]{2,1,0:T(8,128)} custom-call(bf16[2,16,256,128]{3,2,1,0:T(8,128)(2,1)} %bitcast.3, bf16[1024,1024]{1,0:T(8,128)(2,1)} %constant.20.clone.lt_ref), custom_call_target="tpu_custom_call" | custom-call | tf_op jit(solution)/shard_map/lags/pallas_call | solution.py:419
  (1 shorter events, 0.0 us)

commit v3 on v0

v3 whole, which is shorter than its diff:
```python
import functools
import math

import jax
import jax.numpy as jnp
import ml_dtypes
import numpy as np
from jax import lax
from jax.experimental import pallas as pl
from jax.experimental.pallas import tpu as pltpu
from jax.sharding import PartitionSpec as P

WIN = 4096
NFREQ = 512
BANDW = 64
K_LO = 32
LAGS = 1024
TAPS = 32
NW = 24
SRC = 128
BLK = 512
BF = jnp.bfloat16
F32 = jnp.float32
MESH = pl.DeviceIdType.MESH
VLIM = 56 * 1024 * 1024


def split_bf16(a):
    hi = a.astype(ml_dtypes.bfloat16)
    lo = (a - hi.astype(np.float64)).astype(ml_dtypes.bfloat16)
    return hi, lo


def dft_tables():
    u = np.arange(256)[:, None] - 255.5
    ang = 2 * np.pi * u * (np.arange(NFREQ)[None, :] + K_LO) / (2 * WIN)
    out = []
    for t in (np.cos(ang), np.sin(ang)):
        hi, lo = split_bf16(t)
        out.append(np.concatenate([hi, hi, lo], axis=0))
    return np.stack(out)


def twiddles():
    t = np.arange(WIN // BLK)[:, None] * BLK + 255.5
    ang = 2 * np.pi * t * (np.arange(NFREQ)[None, :] + K_LO) / (2 * WIN)
    return np.stack([np.cos(ang), np.sin(ang)], axis=1).astype(np.float32)


def tap_spread():
    j, a, l = np.ogrid[0:TAPS, 0:8, 0:128]
    fwd = (l < 10) & (a - 4 * l + 31 == j)
    rev = (l < 10) & (a - 4 * (9 - l) + 31 == j)
    return np.stack([fwd, rev], axis=1).reshape(TAPS, 2048).astype(ml_dtypes.bfloat16)


def lag_table():
    k = np.arange(NFREQ)[:, None] + K_LO
    i = np.arange(LAGS)[None, :] - LAGS // 2 + 2 * WIN
    ang = 2 * np.pi * ((k * i) % (2 * WIN)) / (2 * WIN)
    t = np.stack([np.cos(ang), -np.sin(ang)]) / math.sqrt(NFREQ * NW)
    t = t.reshape(2, 2, 256, LAGS).transpose(1, 0, 2, 3)
    return t.reshape(2 * NFREQ, LAGS).astype(ml_dtypes.bfloat16)


def band_ones():
    g = np.arange(256) // BANDW
    return (g[:, None] == g[None, :]).astype(ml_dtypes.bfloat16)


def dotf(a, b):
    return jnp.dot(a, b, preferred_element_type=F32)


def tdot(a, b):
    return lax.dot_general(a, b, (((0,), (0,)), ((), ())), preferred_element_type=F32)


def hilo(v):
    hi = v.astype(BF)
    return hi, (v - hi.astype(F32)).astype(BF)


def band_rows(unit, start, lane_tile):
    lane = lax.broadcasted_iota(jnp.int32, (8, 128), 1) + 128 * lane_tile
    lo, hi = 128 * lane_tile, 128 * lane_tile + 127
    if start > hi or start + 9 < lo:
        return jnp.zeros((8, 128), F32)
    moved = pltpu.roll(unit, start % 128, 1) if start % 128 else unit
    return jnp.where((lane >= start) & (lane < start + 10), moved, 0.0)


def build_bands(taps, spread, bands):
    row = dotf(taps, spread)
    for v in range(2):
        unit = jnp.concatenate([row[0:1, (8 * v + a) * 128:(8 * v + a + 1) * 128] for a in range(8)], axis=0)
        for r in range(0, 144, 2):
            starts = [(2 * q - 32) if v == 0 else (278 - 2 * q) for q in (r, r + 1)]
            for t in range(2):
                rows = jnp.concatenate([band_rows(unit, s, t) for s in starts], axis=0)
                bands[v, 8 * r:8 * r + 16, 128 * t:128 * t + 128] = rows.astype(BF)


def swap_blocks(vs):
    lane = lax.broadcasted_iota(jnp.int32, vs[0].shape, 1) // 16
    for bit in (1, 2, 4):
        low = lane & bit == 0
        out = list(vs)
        for i in range(8):
            if i & bit == 0:
                a, b = vs[i], vs[i + bit]
                out[i] = jnp.where(low, a, pltpu.roll(b, 16 * bit, 1))
                out[i + bit] = jnp.where(low, pltpu.roll(a, 128 - 16 * bit, 1), b)
        vs = out
    return vs


def build_left(w, l_buf, u, left):
    odd = (lax.broadcasted_iota(jnp.int32, (16, 128), 1) // 16) % 2 == 1
    for q in range(2):
        for g in range(2):
            vs = []
            for i in range(8):
                m, p = 4 * g + i // 2, i % 2
                vs.append(l_buf[w, m, :, 256 * p + 128 * q:256 * p + 128 * q + 128].astype(F32))
            for j, v in enumerate(swap_blocks(vs)):
                turned = jnp.where(odd, pltpu.roll(v, 16, 1), -pltpu.roll(v, 112, 1))
                u[0, 8 * q + j, :, 128 * g:128 * g + 128] = v
                u[1, 8 * q + j, :, 128 * g:128 * g + 128] = turned
    diag = lax.broadcasted_iota(jnp.int32, (16, 256), 1) % 16 == lax.broadcasted_iota(jnp.int32, (16, 256), 0)

    def expand(j, carry):
        for c in range(16):
            for p in range(2):
                row = jnp.broadcast_to(u[p, j, c:c + 1, :], (16, 256))
                r0 = (2 * c + p) * 16
                left[j, r0:r0 + 16, 256 * w:256 * w + 256] = jnp.where(diag, row, 0.0).astype(BF)
        return carry

    lax.fori_loop(0, 16, expand, 0)


def filter_window(x, bands, lhs, dcat):
    rows = 64
    for b in range(16):
        r0 = (b // 2) * rows
        if b == 0:
            lhs[0, 0:rows, 0:128] = jnp.zeros((rows, 128), BF)
            lhs[0, 0:rows, 128:1152] = x[:, 0:1024]
        else:
            lhs[b % 2, r0:r0 + rows, :] = x[:, 1024 * b - 128:1024 * b + 1024]
    even = dotf(lhs[0], bands[0])
    odd = dotf(lhs[1], bands[1])
    for i, v in enumerate((even + odd, even - odd)):
        hi, lo = hilo(v)
        dcat[i, :, 0:256] = hi
        dcat[i, :, 256:512] = lo
        dcat[i, :, 512:768] = hi


def spectrum_half(h, dcat, tab, tw, ones, sel, wst, picks):
    rows = 64
    cols = slice(256 * h, 256 * h + 256)
    yc = dotf(dcat[0], tab[0, :, cols])
    ys = dotf(dcat[1], tab[1, :, cols])
    xre = xim = 0.0
    for b in range(WIN // BLK):
        c = tw[b, 0:1, cols]
        s = tw[b, 1:2, cols]
        bc = yc[b * rows:(b + 1) * rows]
        bs = ys[b * rows:(b + 1) * rows]
        xre = xre + (bc * c - bs * s)
        xim = xim - (bs * c + bc * s)
    phi, plo = hilo(xre * xre + xim * xim)
    power = dotf(phi, ones[...]) + dotf(plo, ones[...])
    scale = lax.rsqrt(power * (1.0 / BANDW) + 1e-6)
    wre = (xre * scale).astype(BF)
    wim = (xim * scale).astype(BF)
    for z in range(4):
        wst[h, z, :, 0:256] = wre[16 * z:16 * z + 16]
        wst[h, z, :, 256:512] = wim[16 * z:16 * z + 16]
    for p, part in enumerate((wre, wim)):
        picked = tdot(part, sel).astype(BF)
        for j in range(16):
            picks[h, j // 4, j % 4, p] = picked[16 * j:16 * j + 16]


def cross_kernel(x_hbm, tab_hbm, taps_ref, spread_ref, tw, ones, src_ref, xf_ref,
                 x_buf, tab, bands, lhs, dcat, picks, wst, r1, acc, r2, red, zin, s_buf, l_buf, u, left, part, xs,
                 in_sem, p_send, p_recv, z_send, z_recv, t_send, t_recv, l_send, l_recv, l_own, g_send, g_recv,
                 x_sem):
    m = lax.axis_index("tm")
    ch = lax.axis_index("chan")
    core = m % 2
    zl = m // 2
    zh, xy = ch // 16, ch % 16
    x, y = xy // 4, xy % 4
    z = zh * 4 + zl
    barrier = pltpu.get_barrier_semaphore()
    loads = [pltpu.make_async_copy(tab_hbm, tab, in_sem.at[3])]
    loads += [pltpu.make_async_copy(x_hbm.at[w], x_buf.at[w], in_sem.at[w]) for w in range(3)]
    for n in (1, 0, 2, 3):
        loads[n].start()

    def xy_peer(dx, dy):
        return ((x + dx) % 4) * 4 + (y + dy) % 4

    def along(axis, d):
        return (m, zh * 16 + (xy_peer(d, 0) if axis == 0 else xy_peer(0, d)))

    def on_ring(d, to_core):
        zz = (z + d) % 8
        return ((zz % 4) * 2 + to_core, (zz // 4) * 16 + xy)

    for axis in range(2):
        for d in (1, 2, 3):
            pl.semaphore_signal(barrier, inc=1, device_id=along(axis, d), device_id_type=MESH)
    for d in range(8):
        for flip in range(2):
            if d or flip:
                pl.semaphore_signal(barrier, inc=1, device_id=on_ring(d, (core + flip) % 2), device_id_type=MESH)

    def remote(src, dst, ssem, rsem, dev):
        pltpu.make_async_remote_copy(src_ref=src, dst_ref=dst, send_sem=ssem, recv_sem=rsem,
                                     device_id=dev, device_id_type=MESH).start()

    def take(ref, sem):
        pltpu.make_async_copy(ref, ref, sem).wait()

    ids = ch * 64 + lax.broadcasted_iota(jnp.int32, (64, SRC), 0)
    sel = (ids == src_ref[...]).astype(F32).astype(BF)
    build_bands(taps_ref[...], spread_ref[...], bands)
    mine = (x, y)
    arrived = {}

    def mark(w, a, b):
        for f in range(2):
            key = (a, b) if f == 0 else (b, a)
            arrived[w, key] = arrived.get((w, key), 0) + 1
            if arrived[w, key] < 2 or w == 0:
                continue
            j = xy_peer(*key)
            if w == 1:
                part[j] = dotf(left[j, :, 0:512], s_buf[j, 0:2].reshape(512, SRC))
                continue
            o = part[j] + dotf(left[j, :, 512:768], s_buf[j, 2].reshape(256, SRC))
            xs[:, j] = o.astype(BF).reshape(32, 16, SRC)
            remote(xs.at[pl.ds((1 - core) * 16, 16), j], xf_ref.at[core, :, j], x_sem.at[0], x_sem.at[1],
                   (m + 1 - 2 * core, ch))
            pltpu.make_async_copy(xs.at[pl.ds(core * 16, 16), j], xf_ref.at[core, :, j], x_sem.at[2]).start()

    def chain(w):
        def chunk(f, d):
            return picks.at[w, 0, (x + d) % 4] if f == 0 else picks.at[w, 1, :, (y + d) % 4]

        for d in (2, 1, 3):
            for f in range(2):
                remote(chunk(f, d), r1.at[w, f, d - 1], p_send.at[w, 0], p_recv.at[w, 0, f], along(f, d))
        for o in range(1, 8):
            mm = (m + o) % 8
            remote(wst.at[w, mm % 2, mm // 2], l_buf.at[w, m], l_send.at[w], l_recv.at[w], (mm, ch))
        pltpu.make_async_copy(wst.at[w, core, zl], l_buf.at[w, m], l_own.at[w]).start()
        yield
        for f in range(2):
            take(r1.at[w, f], p_recv.at[w, 0, f])
            acc[w, f] = chunk(f, 0)[...] + r1[w, f, 0] + r1[w, f, 1] + r1[w, f, 2]
            for d in (2, 1, 3):
                remote(acc.at[w, f, (mine[1 - f] + d) % 4], r2.at[w, f, d - 1], p_send.at[w, 1],
                       p_recv.at[w, 1, f], along(1 - f, d))
        yield
        for f in range(2):
            take(r2.at[w, f], p_recv.at[w, 1, f])
            red[w, 0, f] = acc[w, f, mine[1 - f]] + r2[w, f, 0] + r2[w, f, 1] + r2[w, f, 2]
        remote(red.at[w, 0], zin.at[w], z_send.at[w], z_recv.at[w], on_ring(4, core))
        yield
        take(zin.at[w], z_recv.at[w])
        red[w, 1] = red[w, 0] + zin[w]
        for d in (2 - 4 * core, 1, -1):
            for flip in range(2):
                to = (core + flip) % 2
                remote(red.at[w, 1, to], s_buf.at[xy, w, m], t_send.at[w], t_recv.at[w], on_ring(d + 8, to))
        remote(red.at[w, 1, 1 - core], s_buf.at[xy, w, m], t_send.at[w], t_recv.at[w], on_ring(0, 1 - core))
        s_buf[xy, w, m] = red[w, 1, core]
        yield
        take(s_buf.at[xy, w, pl.ds(0, 7)], t_recv.at[w])

        def send(f, a, b, slot, d, axis):
            src = xy_peer(a, b) if f == 0 else xy_peer(b, a)
            part = s_buf.at[src, w, pl.ds(4 * f, 4)]
            remote(part, part, g_send.at[w], g_recv.at[w, slot], along(axis, d))

        def second(f, a, slot):
            send(f, a, 0, slot, 1, 1 - f)
            send(f, a, 0, slot, 3, 1 - f)

        def forward(f, a, slot):
            first = 1 if a % 2 == 0 else 3
            send(f, a, 4 - first, slot, first, 1 - f)

        def got(shards, slot):
            take(s_buf.at[pl.ds(0, shards), w], g_recv.at[w, slot])

        for f in range(2):
            send(f, 0, 0, 0, 1, f)
            send(f, 0, 0, 0, 3, f)
        for f in range(2):
            second(f, 0, 2)
        mark(w, 0, 0)
        yield
        got(2, 0)
        for f in range(2):
            first = 1 if f == 0 else 3
            send(f, 4 - first, 0, 1, first, f)
        for f in range(2):
            second(f, 3, 4)
            second(f, 1, 4)
        got(2, 2)
        for f in range(2):
            forward(f, 0, 3)
        for a in (1, 3):
            mark(w, a, 0)
            mark(w, 0, a)
        yield
        got(1, 1)
        for f in range(2):
            second(f, 2, 6)
        got(4, 4)
        for a in (3, 1):
            for f in range(2):
                forward(f, a, 5)
        mark(w, 2, 0)
        for a in (1, 3):
            for b in (1, 3):
                mark(w, a, b)
        yield
        got(2, 6)
        for f in range(2):
            forward(f, 2, 7)
        got(1, 3)
        mark(w, 0, 2)
        got(2, 5)
        for a in (1, 3):
            mark(w, 2, a)
            mark(w, a, 2)
        yield
        got(1, 7)
        mark(w, 2, 2)
        yield

    def filt(w):
        loads[1 + w].wait()
        filter_window(x_buf.at[w], bands, lhs, dcat)

    def half(w, h):
        spectrum_half(h, dcat, tab, tw, ones, sel, wst.at[w], picks.at[w])

    def build(w):
        take(l_buf.at[w, m], l_own.at[w])
        take(l_buf.at[w, pl.ds(0, 7)], l_recv.at[w])
        build_left(w, l_buf, u, left)

    chains = [chain(w) for w in range(3)]

    def go(*ws):
        for w in ws:
            next(chains[w])

    filt(0)
    loads[0].wait()
    half(0, 0)
    half(0, 1)
    pl.semaphore_wait(barrier, 21)
    go(0)
    filt(1)
    half(1, 0)
    half(1, 1)
    go(0, 1)
    filt(2)
    half(2, 0)
    half(2, 1)
    go(0, 2, 1, 2, 1, 0, 2, 0)
    build(0)
    go(1)
    build(1)
    go(0)
    build(2)
    go(1, 2, 0, 2, 1, 2, 1, 0, 2, 1, 2, 0, 1, 2)
    for w in range(3):
        take(r1.at[w], p_send.at[w, 0])
        take(r2.at[w], p_send.at[w, 1])
        take(l_buf.at[w, pl.ds(0, 7)], l_send.at[w])
        take(zin.at[w], z_send.at[w])
        take(s_buf.at[xy, w, pl.ds(0, 7)], t_send.at[w])
        take(s_buf.at[pl.ds(0, 15), w], g_send.at[w])
    for n in range(3):
        take(xs.at[pl.ds(0, 16)], x_sem.at[n])


def cross(x, taps, src):
    vm = pl.BlockSpec(memory_space=pltpu.VMEM)
    hbm = pl.BlockSpec(memory_space=pl.ANY)
    dma = pltpu.SemaphoreType.DMA
    tile = (2, 16, SRC)
    return pl.pallas_call(
        cross_kernel,
        in_specs=[hbm, hbm, vm, vm, vm, vm, vm],
        out_specs=hbm,
        out_shape=jax.ShapeDtypeStruct((2, 16, 16, 16, SRC), BF),
        scratch_shapes=[
            pltpu.VMEM((3, 64, 4 * WIN), BF),
            pltpu.VMEM((2, 768, NFREQ), BF),
            pltpu.VMEM((2, 1152, 256), BF),
            pltpu.VMEM((2, 512, 1152), BF),
            pltpu.VMEM((2, 512, 768), BF),
            pltpu.VMEM((3, 2, 4, 4) + tile, BF),
            pltpu.VMEM((3, 2, 4, 16, 512), BF),
            pltpu.VMEM((3, 2, 3, 4) + tile, BF),
            pltpu.VMEM((3, 2, 4) + tile, BF),
            pltpu.VMEM((3, 2, 3) + tile, BF),
            pltpu.VMEM((3, 2, 2) + tile, BF),
            pltpu.VMEM((3, 2) + tile, BF),
            pltpu.VMEM((16, 3, 8) + tile, BF),
            pltpu.VMEM((3, 8, 16, 512), BF),
            pltpu.VMEM((2, 16, 16, 256), F32),
            pltpu.VMEM((16, 512, 768), BF),
            pltpu.VMEM((16, 512, SRC), F32),
            pltpu.VMEM((32, 16, 16, SRC), BF),
            dma((4,)), dma((3, 2)), dma((3, 2, 2)), dma((3,)), dma((3,)), dma((3,)), dma((3,)), dma((3,)), dma((3,)),
            dma((3,)), dma((3,)), dma((3, 8)), dma((3,)),
        ],
        compiler_params=pltpu.CompilerParams(collective_id=0, has_side_effects=True, vmem_limit_bytes=VLIM),
        name="cross",
    )(x, jnp.asarray(dft_tables()), taps, jnp.asarray(tap_spread()), jnp.asarray(twiddles()),
      jnp.asarray(band_ones()), src)


def lags_kernel(xf_ref, lt_ref, out_ref, lhs):
    @pl.when(pl.program_id(0) == 0)
    def _():
        for c in range(8):
            lhs[c * SRC:(c + 1) * SRC, :] = xf_ref[:, 2 * c:2 * c + 2].reshape(1024, SRC).T

    o = dotf(lhs[...], lt_ref[...])
    for c in range(8):
        out_ref[:, c, :] = o[c * SRC:(c + 1) * SRC]


def lags(xf):
    return pl.pallas_call(
        lags_kernel,
        grid=(4,),
        in_specs=[
            pl.BlockSpec((2, 16, 256, SRC), lambda n: (0, 0, 0, 0)),
            pl.BlockSpec((1024, 256), lambda n: (0, n)),
        ],
        out_specs=pl.BlockSpec((SRC, 8, 256), lambda n: (0, 0, n)),
        out_shape=jax.ShapeDtypeStruct((SRC, 8, LAGS), F32),
        scratch_shapes=[pltpu.VMEM((1024, 1024), BF)],
        compiler_params=pltpu.CompilerParams(vmem_limit_bytes=VLIM),
        name="lags",
    )(xf, jnp.asarray(lag_table()))


def on_device(strain_rate, fir_taps, source_channels):
    x = jnp.transpose(strain_rate, (1, 0, 2))
    xf = cross(x, fir_taps.reshape(1, TAPS), source_channels.reshape(1, SRC))
    return lags(xf.reshape(2, 16, 256, SRC))


def solution(mesh):
    placed = (P("chan", "tm", None), P(), P())
    return jax.shard_map(
        on_device,
        mesh=mesh,
        in_specs=placed,
        out_specs=P(None, ("chan", "tm"), None),
        check_vma=False,
    )
```

time: 826 us -> 63.3 us (0.08)
  waiting for transfers between devices: 560 us -> 0 us
  matrix products: 96.1 us -> 0 us
  local copies, waits for them, and re-layouts: 85.6 us -> 0 us
  Pallas kernels: 0 us -> 63.1 us
  other arithmetic: 56.1 us -> 0 us
  between operations: 13.5 us -> 0.01 us
    psum x1 -> x0, waiting for transfers between devices: 479 us -> none  [on_device(): lax.psum(collected.astype(jnp.float32).astype(jnp.bfloat16), 'chan')]
    all_gather x1 -> x0, waiting for transfers between devices: 75.9 us -> none  [on_device(): lax.all_gather(selection.astype(jnp.bfloat16), 'tm', axis=1, tiled=True)]
    pallas_call x0 -> x2, Pallas kernels: none -> 63.1 us  [the longest x1 55.9 us: cross(): pl.pallas_call(cross_kernel, in_specs=[hbm, hbm, vm, vm, vm, vm, vm], out...]
    conv_general_dilated x1 -> x0, matrix products: 56.6 us -> none  [whiten(): lax.conv_general_dilated(signal, kernel, (4,), [(fir_taps.shape[0] - 1, 0...]
    cos x2 -> x0, other arithmetic: 46.7 us -> none  [the longest x1 36.8 us: forward_table(): return jnp.concatenate([jnp.cos(angles), -jnp.sin(angles)], axis=1)]
    reshape x3 -> x0, local copies, waits for them, and re-layouts: 44.4 us -> none  [the longest x2 44.3 us: whiten(): signal = records.reshape(channels * windows, 1, samples)]
    dot_general x7 -> x0, matrix products: 39.5 us -> none  [the longest x1 17.4 us: correlate(): jnp.dot(flattened, table, precision=lax.Precision.HIGHEST, preferred_elem...]
    unnamed x16 -> x0, local copies, waits for them, and re-layouts: 20.1 us -> none
  transfers between devices with their start and end apart: 3 -> 0, of which waited for: 3 -> 0; matrix products, arithmetic and copies ran while one was open for 2% -> 0% of each run, Pallas kernels for 0% -> 0%
where the time goes in v3:
time: 63.3 us; the launch traced here: 63.1 us
  Pallas kernels  63.1 us (100%)
    pallas_call x1, Pallas kernels, cross(): pl.pallas_call(cross_kernel, in_specs=[hbm, hbm, vm, vm, vm, vm, vm], out...  55.9 us
    pallas_call x1, Pallas kernels, lags(): pl.pallas_call(lags_kernel, grid=(4,), in_specs=[pl.BlockSpec((2, 16, 256...  7.26 us

profile of v3, /device:TPU:1, one launch (start us, length us, event | category | flops | bytes accessed | tf_op | source)
XLA Modules:
  0.0 63.1 jit_solution(13240378597757745697)
XLA Ops:
  0.0 55.9 %cross.1 = bf16[2,16,16,16,128]{4,3,2,1,0:T(8,128)(2,1)} custom-call(bf16[3,64,16384]{2,1,0:T(8,128)(2,1)} %bitcast.5, bf16[2,768,512]{2,1,0:T(8,128)(2,1)} %constant.10.clone.tab_hbm, bf16[1,32]{1,0:T(2,128)(2,1)} %bitcast.6, bf16[32,2048]{1,0:T(8,128)(2,1)} %constant.11.clone.spread_ref, f32[8,2,512]{2,1,0:T(2,128)} %constant.12.clone.tw, ...), custom_call_target="tpu_custom_call" | custom-call | tf_op jit(solution)/shard_map/cross/pallas_call | solution.py:404
  55.9 7.3 %lags.1 = f32[128,8,1024]{2,1,0:T(8,128)} custom-call(bf16[2,16,256,128]{3,2,1,0:T(8,128)(2,1)} %bitcast.4, bf16[1024,1024]{1,0:T(8,128)(2,1)} %constant.14.clone.lt_ref), custom_call_target="tpu_custom_call" | custom-call | tf_op jit(solution)/shard_map/lags/pallas_call | solution.py:449

commit v4 on v3

--- a/solution.py
+++ b/solution.py
@@ -19,6 +19,7 @@
 NW = 24
 SRC = 128
 BLK = 512
+TABLE_ROWS = 10240
 BF = jnp.bfloat16
 F32 = jnp.float32
 MESH = pl.DeviceIdType.MESH
@@ -51,7 +52,19 @@
     j, a, l = np.ogrid[0:TAPS, 0:8, 0:128]
     fwd = (l < 10) & (a - 4 * l + 31 == j)
     rev = (l < 10) & (a - 4 * (9 - l) + 31 == j)
-    return np.stack([fwd, rev], axis=1).reshape(TAPS, 2048).astype(ml_dtypes.bfloat16)
+    return np.stack([fwd, rev], axis=1).reshape(TAPS, 4, 512).transpose(1, 0, 2).reshape(4 * TAPS, 512)
+
+
+def tables():
+    tw = twiddles().reshape(16, NFREQ).astype(np.float64)
+    hi, rest = split_bf16(tw)
+    mid, lo = split_bf16(tw - hi.astype(np.float64))
+    rows = np.zeros((TABLE_ROWS, NFREQ), ml_dtypes.bfloat16)
+    rows[0:1536] = dft_tables().reshape(1536, NFREQ)
+    rows[1536:1792, 0:256] = band_ones()
+    rows[1792:1920] = tap_spread()
+    rows[1920:1968] = np.concatenate([hi, mid, lo])
+    return rows
 
 
 def lag_table():
@@ -59,7 +72,7 @@
     i = np.arange(LAGS)[None, :] - LAGS // 2 + 2 * WIN
     ang = 2 * np.pi * ((k * i) % (2 * WIN)) / (2 * WIN)
     t = np.stack([np.cos(ang), -np.sin(ang)]) / math.sqrt(NFREQ * NW)
-    t = t.reshape(2, 2, 256, LAGS).transpose(1, 0, 2, 3)
+    t = t.reshape(2, 2, 16, 16, LAGS).transpose(1, 2, 0, 3, 4)
     return t.reshape(2 * NFREQ, LAGS).astype(ml_dtypes.bfloat16)
 
 
@@ -91,7 +104,7 @@
 
 
 def build_bands(taps, spread, bands):
-    row = dotf(taps, spread)
+    row = jnp.concatenate([dotf(taps, spread[TAPS * n:TAPS * n + TAPS]) for n in range(4)], axis=1)
     for v in range(2):
         unit = jnp.concatenate([row[0:1, (8 * v + a) * 128:(8 * v + a + 1) * 128] for a in range(8)], axis=0)
         for r in range(0, 144, 2):
@@ -161,18 +174,18 @@
 def spectrum_half(h, dcat, tab, tw, ones, sel, wst, picks):
     rows = 64
     cols = slice(256 * h, 256 * h + 256)
-    yc = dotf(dcat[0], tab[0, :, cols])
-    ys = dotf(dcat[1], tab[1, :, cols])
+    yc = dotf(dcat[0], tab[0:768, cols])
+    ys = dotf(dcat[1], tab[768:1536, cols])
     xre = xim = 0.0
     for b in range(WIN // BLK):
-        c = tw[b, 0:1, cols]
-        s = tw[b, 1:2, cols]
+        c = tw[2 * b:2 * b + 1, cols]
+        s = tw[2 * b + 1:2 * b + 2, cols]
         bc = yc[b * rows:(b + 1) * rows]
         bs = ys[b * rows:(b + 1) * rows]
         xre = xre + (bc * c - bs * s)
         xim = xim - (bs * c + bc * s)
     phi, plo = hilo(xre * xre + xim * xim)
-    power = dotf(phi, ones[...]) + dotf(plo, ones[...])
+    power = dotf(phi, ones) + dotf(plo, ones)
     scale = lax.rsqrt(power * (1.0 / BANDW) + 1e-6)
     wre = (xre * scale).astype(BF)
     wim = (xim * scale).astype(BF)
@@ -185,8 +198,7 @@
             picks[h, j // 4, j % 4, p] = picked[16 * j:16 * j + 16]
 
 
-def cross_kernel(x_hbm, tab_hbm, taps_ref, spread_ref, tw, ones, src_ref, xf_ref,
-                 x_buf, tab, bands, lhs, dcat, picks, wst, r1, acc, r2, red, zin, s_buf, l_buf, u, left, part, xs,
+def cross_kernel(x_hbm, rows_hbm, small, xf_ref, x_buf, tab, aux, tw, bands, lhs, dcat, picks, wst, r1, acc, r2, red, zin, s_buf, l_buf, u, left, part, xs,
                  in_sem, p_send, p_recv, z_send, z_recv, t_send, t_recv, l_send, l_recv, l_own, g_send, g_recv,
                  x_sem):
     m = lax.axis_index("tm")
@@ -197,10 +209,11 @@
     x, y = xy // 4, xy % 4
     z = zh * 4 + zl
     barrier = pltpu.get_barrier_semaphore()
-    loads = [pltpu.make_async_copy(tab_hbm, tab, in_sem.at[3])]
+    loads = [pltpu.make_async_copy(rows_hbm.at[pl.ds(0, 1536)], tab, in_sem.at[3])]
     loads += [pltpu.make_async_copy(x_hbm.at[w], x_buf.at[w], in_sem.at[w]) for w in range(3)]
-    for n in (1, 0, 2, 3):
-        loads[n].start()
+    aux_load = pltpu.make_async_copy(rows_hbm.at[pl.ds(1536, 432)], aux, in_sem.at[4])
+    for c in [aux_load, loads[1], loads[0]] + loads[2:]:
+        c.start()
 
     def xy_peer(dx, dy):
         return ((x + dx) % 4) * 4 + (y + dy) % 4
@@ -227,27 +240,33 @@
     def take(ref, sem):
         pltpu.make_async_copy(ref, ref, sem).wait()
 
-    ids = ch * 64 + lax.broadcasted_iota(jnp.int32, (64, SRC), 0)
-    sel = (ids == src_ref[...]).astype(F32).astype(BF)
-    build_bands(taps_ref[...], spread_ref[...], bands)
+    aux_load.wait()
+    ids = (ch * 64 + lax.broadcasted_iota(jnp.int32, (64, SRC), 0)).astype(F32)
+    sel = jnp.maximum(1.0 - jnp.abs(ids - small[1:2, :]), 0.0).astype(BF)
+    tw[...] = aux[384:400].astype(F32) + aux[400:416].astype(F32) + aux[416:432].astype(F32)
+    ones = aux[0:256, 0:256]
+    build_bands(small[0:1, 0:TAPS].astype(BF), aux[256:384], bands)
     mine = (x, y)
     arrived = {}
 
-    def mark(w, a, b):
-        for f in range(2):
-            key = (a, b) if f == 0 else (b, a)
-            arrived[w, key] = arrived.get((w, key), 0) + 1
-            if arrived[w, key] < 2 or w == 0:
-                continue
-            j = xy_peer(*key)
-            if w == 1:
+    def mark(w, *keys):
+        ready = []
+        for a, b in keys:
+            for f in range(2):
+                key = (a, b) if f == 0 else (b, a)
+                arrived[w, key] = arrived.get((w, key), 0) + 1
+                if arrived[w, key] == 2:
+                    ready.append(xy_peer(*key))
+        if w == 1:
+            for j in ready:
                 part[j] = dotf(left[j, :, 0:512], s_buf[j, 0:2].reshape(512, SRC))
-                continue
-            o = part[j] + dotf(left[j, :, 512:768], s_buf[j, 2].reshape(256, SRC))
-            xs[:, j] = o.astype(BF).reshape(32, 16, SRC)
-            remote(xs.at[pl.ds((1 - core) * 16, 16), j], xf_ref.at[core, :, j], x_sem.at[0], x_sem.at[1],
-                   (m + 1 - 2 * core, ch))
-            pltpu.make_async_copy(xs.at[pl.ds(core * 16, 16), j], xf_ref.at[core, :, j], x_sem.at[2]).start()
+        if w == 2:
+            for j in ready:
+                o = part[j] + dotf(left[j, :, 512:768], s_buf[j, 2].reshape(256, SRC))
+                xs[:, j] = o.astype(BF).reshape(2, 16, 16, SRC)
+            for j in ready:
+                remote(xs.at[1 - core, j], xf_ref.at[core, j], x_sem.at[0], x_sem.at[1], (m + 1 - 2 * core, ch))
+                pltpu.make_async_copy(xs.at[core, j], xf_ref.at[core, j], x_sem.at[2]).start()
 
     def chain(w):
         def chunk(f, d):
@@ -305,7 +324,7 @@
             send(f, 0, 0, 0, 3, f)
         for f in range(2):
             second(f, 0, 2)
-        mark(w, 0, 0)
+        mark(w, (0, 0))
         yield
         got(2, 0)
         for f in range(2):
@@ -317,9 +336,7 @@
         got(2, 2)
         for f in range(2):
             forward(f, 0, 3)
-        for a in (1, 3):
-            mark(w, a, 0)
-            mark(w, 0, a)
+        mark(w, (1, 0), (0, 1), (3, 0), (0, 3))
         yield
         got(1, 1)
         for f in range(2):
@@ -328,23 +345,17 @@
         for a in (3, 1):
             for f in range(2):
                 forward(f, a, 5)
-        mark(w, 2, 0)
-        for a in (1, 3):
-            for b in (1, 3):
-                mark(w, a, b)
+        mark(w, (2, 0), (1, 1), (1, 3), (3, 1), (3, 3))
         yield
         got(2, 6)
         for f in range(2):
             forward(f, 2, 7)
         got(1, 3)
-        mark(w, 0, 2)
         got(2, 5)
-        for a in (1, 3):
-            mark(w, 2, a)
-            mark(w, a, 2)
+        mark(w, (0, 2), (2, 1), (1, 2), (2, 3), (3, 2))
         yield
         got(1, 7)
-        mark(w, 2, 2)
+        mark(w, (2, 2))
         yield
 
     def filt(w):
@@ -393,22 +404,23 @@
         take(s_buf.at[xy, w, pl.ds(0, 7)], t_send.at[w])
         take(s_buf.at[pl.ds(0, 15), w], g_send.at[w])
     for n in range(3):
-        take(xs.at[pl.ds(0, 16)], x_sem.at[n])
-
-
-def cross(x, taps, src):
-    vm = pl.BlockSpec(memory_space=pltpu.VMEM)
-    hbm = pl.BlockSpec(memory_space=pl.ANY)
+        take(xs.at[0], x_sem.at[n])
+
+
+def cross(x, small):
+    hbm = pl.BlockSpec(memory_space=pltpu.HBM)
     dma = pltpu.SemaphoreType.DMA
     tile = (2, 16, SRC)
     return pl.pallas_call(
         cross_kernel,
-        in_specs=[hbm, hbm, vm, vm, vm, vm, vm],
-        out_specs=hbm,
+        in_specs=[hbm, hbm, pl.BlockSpec(memory_space=pltpu.VMEM)],
+        out_specs=pl.BlockSpec(memory_space=pl.ANY),
         out_shape=jax.ShapeDtypeStruct((2, 16, 16, 16, SRC), BF),
         scratch_shapes=[
             pltpu.VMEM((3, 64, 4 * WIN), BF),
-            pltpu.VMEM((2, 768, NFREQ), BF),
+            pltpu.VMEM((1536, NFREQ), BF),
+            pltpu.VMEM((432, NFREQ), BF),
+            pltpu.VMEM((16, NFREQ), F32),
             pltpu.VMEM((2, 1152, 256), BF),
             pltpu.VMEM((2, 512, 1152), BF),
             pltpu.VMEM((2, 512, 768), BF),
@@ -424,21 +436,20 @@
             pltpu.VMEM((2, 16, 16, 256), F32),
             pltpu.VMEM((16, 512, 768), BF),
             pltpu.VMEM((16, 512, SRC), F32),
-            pltpu.VMEM((32, 16, 16, SRC), BF),
-            dma((4,)), dma((3, 2)), dma((3, 2, 2)), dma((3,)), dma((3,)), dma((3,)), dma((3,)), dma((3,)), dma((3,)),
+            pltpu.VMEM((2, 16, 16, 16, SRC), BF),
+            dma((5,)), dma((3, 2)), dma((3, 2, 2)), dma((3,)), dma((3,)), dma((3,)), dma((3,)), dma((3,)), dma((3,)),
             dma((3,)), dma((3,)), dma((3, 8)), dma((3,)),
         ],
-        compiler_params=pltpu.CompilerParams(collective_id=0, has_side_effects=True, vmem_limit_bytes=VLIM),
+        compiler_params=pltpu.CompilerParams(collective_id=0, has_side_effects=True, vmem_limit_bytes=50 << 20),
         name="cross",
-    )(x, jnp.asarray(dft_tables()), taps, jnp.asarray(tap_spread()), jnp.asarray(twiddles()),
-      jnp.asarray(band_ones()), src)
+    )(x, jnp.asarray(tables()), small)
 
 
 def lags_kernel(xf_ref, lt_ref, out_ref, lhs):
     @pl.when(pl.program_id(0) == 0)
     def _():
         for c in range(8):
-            lhs[c * SRC:(c + 1) * SRC, :] = xf_ref[:, 2 * c:2 * c + 2].reshape(1024, SRC).T
+            lhs[c * SRC:(c + 1) * SRC, :] = xf_ref[:, :, 2 * c:2 * c + 2].reshape(1024, SRC).T
 
     o = dotf(lhs[...], lt_ref[...])
     for c in range(8):
@@ -450,21 +461,23 @@
         lags_kernel,
         grid=(4,),
         in_specs=[
-            pl.BlockSpec((2, 16, 256, SRC), lambda n: (0, 0, 0, 0)),
+            pl.BlockSpec((2, 16, 16, 16, SRC), lambda n: (0, 0, 0, 0, 0)),
             pl.BlockSpec((1024, 256), lambda n: (0, n)),
         ],
         out_specs=pl.BlockSpec((SRC, 8, 256), lambda n: (0, 0, n)),
         out_shape=jax.ShapeDtypeStruct((SRC, 8, LAGS), F32),
         scratch_shapes=[pltpu.VMEM((1024, 1024), BF)],
-        compiler_params=pltpu.CompilerParams(vmem_limit_bytes=VLIM),
+        compiler_params=pltpu.CompilerParams(vmem_limit_bytes=24 << 20),
         name="lags",
     )(xf, jnp.asarray(lag_table()))
 
 
 def on_device(strain_rate, fir_taps, source_channels):
     x = jnp.transpose(strain_rate, (1, 0, 2))
-    xf = cross(x, fir_taps.reshape(1, TAPS), source_channels.reshape(1, SRC))
-    return lags(xf.reshape(2, 16, 256, SRC))
+    taps = jnp.pad(fir_taps.astype(F32), (0, SRC - TAPS))
+    first = lax.broadcasted_iota(jnp.int32, (2, SRC), 0) == 0
+    xf = cross(x, jnp.where(first, taps[None, :], source_channels.astype(F32)[None, :]))
+    return lags(xf)
 
 
 def solution(mesh):

time: 63.3 us -> 62 us (0.979)
  Pallas kernels: 63.1 us -> 60.5 us
  other arithmetic: 0 us -> 1.39 us
    pallas_call x2, Pallas kernels: 63.1 us -> 60.5 us  [the longest x1 55.3 us: cross(): pl.pallas_call(cross_kernel, in_specs=[hbm, hbm, pl.BlockSpec(memory_spac...]
    pad x0 -> x1, other arithmetic: none -> 0.66 us  [on_device(): taps = jnp.pad(fir_taps.astype(F32), (0, SRC - TAPS))]
    convert_element_type x0 -> x1, other arithmetic: none -> 0.66 us  [on_device(): source_channels.astype(F32)[None, :]]
where the time goes in v4:
time: 62 us; the launch traced here: 61.9 us
  Pallas kernels  60.5 us (98%)
  other arithmetic  1.39 us (2%)
    pallas_call x1, Pallas kernels, cross(): pl.pallas_call(cross_kernel, in_specs=[hbm, hbm, pl.BlockSpec(memory_spac...  55.3 us
    pallas_call x1, Pallas kernels, lags(): pl.pallas_call(lags_kernel, grid=(4,), in_specs=[pl.BlockSpec((2, 16, 16,...  5.2 us

profile of v4, /device:TPU:1, one launch (start us, length us, event | category | flops | bytes accessed | tf_op | source)
XLA Modules:
  0.0 61.9 jit_solution(8141320378304647525)
XLA Ops:
  0.0 0.7 %pad_convert_fusion = f32[128]{0:T(128)S(1)} fusion(bf16[32]{0:T(256)(128)(2,1)} %param.6), kind=kLoop, calls=%fused_computation.1 | loop fusion | flops 128 | bytes 576 | tf_op jit(solution)/shard_map/jit(_pad)/pad | solution.py:477
  0.7 0.7 %convert_element_type.6 = f32[128]{0:T(128)S(1)} convert(s32[128]{0:T(128)} %param.7) | non-fusion elementwise | flops 128 | bytes 1024 | tf_op jit(solution)/shard_map/convert_element_type | solution.py:479
  1.3 0.1 broadcast_select_fusion.small
  1.4 0.0 copy-start
  1.4 55.3 %cross.1.xf_ref = bf16[2,16,16,16,128]{4,3,2,1,0:T(8,128)(2,1)S(1)} custom-call(bf16[3,64,16384]{2,1,0:T(8,128)(2,1)} %bitcast.1, bf16[10240,512]{1,0:T(8,128)(2,1)} %constant.10.clone.rows_hbm, f32[2,128]{1,0:T(2,128)S(1)} %broadcast_select_fusion.small), custom_call_target="tpu_custom_call" | custom-call | tf_op jit(solution)/shard_map/cross/pallas_call | solution.py:414
  56.7 0.0 copy-done
  56.7 5.2 %lags.1 = f32[128,8,1024]{2,1,0:T(8,128)} custom-call(bf16[2,16,16,16,128]{4,3,2,1,0:T(8,128)(2,1)S(1)} %cross.1.xf_ref, bf16[1024,1024]{1,0:T(8,128)(2,1)S(1)} %copy-done), custom_call_target="tpu_custom_call" | custom-call | tf_op jit(solution)/shard_map/lags/pallas_call | solution.py:460
  (1 shorter events, 0.0 us)
Async XLA Ops:
  1.4 55.3 %copy-start = (bf16[1024,1024]{1,0:T(8,128)(2,1)S(1)}, bf16[1024,1024]{1,0:T(8,128)(2,1)}, u32[]{:S(2)}) copy-start(bf16[1024,1024]{1,0:T(8,128)(2,1)} %constant.11.clone.lt_ref) | copy-start | bytes 6291460

commit v5 on v4

--- a/solution.py
+++ b/solution.py
@@ -445,28 +445,33 @@
     )(x, jnp.asarray(tables()), small)
 
 
-def lags_kernel(xf_ref, lt_ref, out_ref, lhs):
-    @pl.when(pl.program_id(0) == 0)
-    def _():
+def lags_kernel(xf_ref, lt_ref, out_hbm, lhs, blocks, sems):
+    for c in range(8):
+        lhs[c * SRC:(c + 1) * SRC, :] = xf_ref[:, :, 2 * c:2 * c + 2].reshape(1024, SRC).T
+    writes = []
+    for n in range(4):
+        cols = pl.ds(256 * n, 256)
+        o = dotf(lhs[...], lt_ref[:, cols])
         for c in range(8):
-            lhs[c * SRC:(c + 1) * SRC, :] = xf_ref[:, :, 2 * c:2 * c + 2].reshape(1024, SRC).T
-
-    o = dotf(lhs[...], lt_ref[...])
-    for c in range(8):
-        out_ref[:, c, :] = o[c * SRC:(c + 1) * SRC]
+            blocks[n, :, c, :] = o[c * SRC:(c + 1) * SRC]
+        writes.append(pltpu.make_async_copy(blocks.at[n], out_hbm.at[:, :, cols], sems.at[n]))
+        writes[n].start()
+    for w in writes:
+        w.wait()
 
 
 def lags(xf):
+    vm = pl.BlockSpec(memory_space=pltpu.VMEM)
     return pl.pallas_call(
         lags_kernel,
-        grid=(4,),
-        in_specs=[
-            pl.BlockSpec((2, 16, 16, 16, SRC), lambda n: (0, 0, 0, 0, 0)),
-            pl.BlockSpec((1024, 256), lambda n: (0, n)),
+        in_specs=[vm, vm],
+        out_specs=pl.BlockSpec(memory_space=pltpu.HBM),
+        out_shape=jax.ShapeDtypeStruct((SRC, 8, LAGS), F32),
+        scratch_shapes=[
+            pltpu.VMEM((1024, 1024), BF),
+            pltpu.VMEM((4, SRC, 8, 256), F32),
+            pltpu.SemaphoreType.DMA((4,)),
         ],
-        out_specs=pl.BlockSpec((SRC, 8, 256), lambda n: (0, 0, n)),
-        out_shape=jax.ShapeDtypeStruct((SRC, 8, LAGS), F32),
-        scratch_shapes=[pltpu.VMEM((1024, 1024), BF)],
         compiler_params=pltpu.CompilerParams(vmem_limit_bytes=24 << 20),
         name="lags",
     )(xf, jnp.asarray(lag_table()))

time: 62 us -> 61.5 us (level)
  Pallas kernels: 60.5 us -> 59.8 us
    pallas_call x1, Pallas kernels: 5.2 us -> 4.55 us  [lags(): pl.pallas_call(lags_kernel, in_specs=[vm, vm], out_specs=pl.BlockSpec(mem...]
where the time goes in v5:
time: 61.5 us; the launch traced here: 61.4 us
  Pallas kernels  59.8 us (97%)
  other arithmetic  1.39 us (2%)
    pallas_call x1, Pallas kernels, cross(): pl.pallas_call(cross_kernel, in_specs=[hbm, hbm, pl.BlockSpec(memory_spac...  55.3 us
    pallas_call x1, Pallas kernels, lags(): pl.pallas_call(lags_kernel, in_specs=[vm, vm], out_specs=pl.BlockSpec(mem...  4.55 us

profile of v5, /device:TPU:1, one launch (start us, length us, event | category | flops | bytes accessed | tf_op | source)
XLA Modules:
  0.0 61.4 jit_solution(7857956629082131310)
XLA Ops:
  0.0 0.7 %pad_convert_fusion = f32[128]{0:T(128)S(1)} fusion(bf16[32]{0:T(256)(128)(2,1)} %param.6), kind=kLoop, calls=%fused_computation.1 | loop fusion | flops 128 | bytes 576 | tf_op jit(solution)/shard_map/jit(_pad)/pad | solution.py:482
  0.7 0.7 %convert_element_type.6 = f32[128]{0:T(128)S(1)} convert(s32[128]{0:T(128)} %param.7) | non-fusion elementwise | flops 128 | bytes 1024 | tf_op jit(solution)/shard_map/convert_element_type | solution.py:484
  1.3 0.1 broadcast_select_fusion.small
  1.4 0.0 copy-start
  1.4 55.3 %cross.1.xf_ref = bf16[2,16,16,16,128]{4,3,2,1,0:T(8,128)(2,1)S(1)} custom-call(bf16[3,64,16384]{2,1,0:T(8,128)(2,1)} %bitcast.1, bf16[10240,512]{1,0:T(8,128)(2,1)} %constant.10.clone.rows_hbm, f32[2,128]{1,0:T(2,128)S(1)} %broadcast_select_fusion.small), custom_call_target="tpu_custom_call" | custom-call | tf_op jit(solution)/shard_map/cross/pallas_call | solution.py:414
  56.7 0.0 copy-done
  56.7 4.5 %lags.1 = f32[128,8,1024]{2,1,0:T(8,128)} custom-call(bf16[2,16,16,16,128]{4,3,2,1,0:T(8,128)(2,1)S(1)} %cross.1.xf_ref, bf16[1024,1024]{1,0:T(8,128)(2,1)S(1)} %copy-done), custom_call_target="tpu_custom_call" | custom-call | tf_op jit(solution)/shard_map/lags/pallas_call | solution.py:465
  (1 shorter events, 0.0 us)
Async XLA Ops:
  1.4 55.3 %copy-start = (bf16[1024,1024]{1,0:T(8,128)(2,1)S(1)}, bf16[1024,1024]{1,0:T(8,128)(2,1)}, u32[]{:S(2)}) copy-start(bf16[1024,1024]{1,0:T(8,128)(2,1)} %constant.11.clone.lt_ref) | copy-start | bytes 6291460

commit v6 on v5

--- a/solution.py
+++ b/solution.py
@@ -328,7 +328,7 @@
         yield
         got(2, 0)
         for f in range(2):
-            first = 1 if f == 0 else 3
+            first = 1 if (f + w) % 2 == 0 else 3
             send(f, 4 - first, 0, 1, first, f)
         for f in range(2):
             second(f, 3, 4)

time: 61.5 us -> 61.8 us (level)
  no operation moved by 1% of the time
where the time goes in v6:
time: 61.8 us; the launch traced here: 61.7 us
  Pallas kernels  60.1 us (97%)
  other arithmetic  1.39 us (2%)
    pallas_call x1, Pallas kernels, cross(): pl.pallas_call(cross_kernel, in_specs=[hbm, hbm, pl.BlockSpec(memory_spac...  55.6 us
    pallas_call x1, Pallas kernels, lags(): pl.pallas_call(lags_kernel, in_specs=[vm, vm], out_specs=pl.BlockSpec(mem...  4.55 us

profile of v6, /device:TPU:1, one launch (start us, length us, event | category | flops | bytes accessed | tf_op | source)
XLA Modules:
  0.0 61.7 jit_solution(12576512445900311425)
XLA Ops:
  0.0 0.7 %pad_convert_fusion = f32[128]{0:T(128)S(1)} fusion(bf16[32]{0:T(256)(128)(2,1)} %param.6), kind=kLoop, calls=%fused_computation.1 | loop fusion | flops 128 | bytes 576 | tf_op jit(solution)/shard_map/jit(_pad)/pad | solution.py:482
  0.7 0.7 %convert_element_type.6 = f32[128]{0:T(128)S(1)} convert(s32[128]{0:T(128)} %param.7) | non-fusion elementwise | flops 128 | bytes 1024 | tf_op jit(solution)/shard_map/convert_element_type | solution.py:484
  1.3 0.1 broadcast_select_fusion.small
  1.4 0.0 copy-start
  1.4 55.6 %cross.1.xf_ref = bf16[2,16,16,16,128]{4,3,2,1,0:T(8,128)(2,1)S(1)} custom-call(bf16[3,64,16384]{2,1,0:T(8,128)(2,1)} %bitcast.1, bf16[10240,512]{1,0:T(8,128)(2,1)} %constant.10.clone.rows_hbm, f32[2,128]{1,0:T(2,128)S(1)} %broadcast_select_fusion.small), custom_call_target="tpu_custom_call" | custom-call | tf_op jit(solution)/shard_map/cross/pallas_call | solution.py:414
  57.0 0.0 copy-done
  57.0 4.6 %lags.1 = f32[128,8,1024]{2,1,0:T(8,128)} custom-call(bf16[2,16,16,16,128]{4,3,2,1,0:T(8,128)(2,1)S(1)} %cross.1.xf_ref, bf16[1024,1024]{1,0:T(8,128)(2,1)S(1)} %copy-done), custom_call_target="tpu_custom_call" | custom-call | tf_op jit(solution)/shard_map/lags/pallas_call | solution.py:465
  (1 shorter events, 0.0 us)
Async XLA Ops:
  1.4 55.6 %copy-start = (bf16[1024,1024]{1,0:T(8,128)(2,1)S(1)}, bf16[1024,1024]{1,0:T(8,128)(2,1)}, u32[]{:S(2)}) copy-start(bf16[1024,1024]{1,0:T(8,128)(2,1)} %constant.11.clone.lt_ref) | copy-start | bytes 6291460
